TPU v7x, 1024 devices: a whole 4x4x32 slice. The times are simulated.
1024 devices in a mesh: dp: 32 (over x, z_hi, core), mx: 4 (over y), my: 8 (over z_lo).
Axes of the slice: x: 4, y: 4, z: 32 (z_hi: 4, z_lo: 8; z = z_hi * 8 + z_lo), core: 2. Of those that a mesh axis runs over, the one named last changes fastest.
Arguments:
- saved_block_input: bfloat16 [8192, 6144], P('dp', 'mx'), may hold values from -6 to 6
- token_row_mean: float32 [8192], P('dp'), may hold values from -3 to 3
- qk_weight: bfloat16 [6144, 2, 3072], P('mx', None, 'my'), may hold values from -0.078125 to 0.078125
- norm_grads: bfloat16 [8192, 2, 3072], P('dp', None, 'my'), may hold values from -6 to 6
Outputs:
- block_input_gradient: bfloat16 [8192, 6144], P(('dp', 'my'), 'mx')
- weight_grad: float32 [6144, 2, 3072], P(('mx', 'dp'), None, 'my')
All inputs are finite; a program needn't handle non-finite values.
Results may differ from a plain program's by a relative error of at most 0.02.
Values may be sent and summed in bfloat16 or wider, within the bound.
No kernel may reach another device: no remote copies, remote signals or barrier semaphores. Data moves between devices by JAX's collectives and lax.ppermute only.
A program may use at most 32 MiB of HBM per device.

v0:
```python
import jax
import jax.numpy as jnp
from jax import lax
from jax.sharding import PartitionSpec as P

D = 6144
HEAD_DIM = 128


def head_norm_back(raw, grads):
    rows = raw.shape[0]
    shaped = raw.reshape(rows, 2, -1, HEAD_DIM)
    upstream = grads.astype(jnp.float32).reshape(rows, 2, -1, HEAD_DIM)
    centre = jnp.mean(shaped, axis=-1, keepdims=True)
    spread = lax.rsqrt(jnp.mean((shaped - centre) ** 2, axis=-1, keepdims=True) + 1e-06)
    normal = (shaped - centre) * spread
    mean_grad = jnp.mean(upstream, axis=-1, keepdims=True)
    mean_cross = jnp.mean(upstream * normal, axis=-1, keepdims=True)
    d_raw = spread * (upstream - mean_grad - normal * mean_cross)
    return d_raw.reshape(rows, -1).astype(jnp.bfloat16)


def per_device(saved_block_input, token_row_mean, qk_weight, norm_grads):
    tokens, width = saved_block_input.shape
    cols = qk_weight.shape[2]
    normed_rows = (saved_block_input.astype(jnp.float32) - token_row_mean[:, None]).astype(
        jnp.bfloat16
    )
    flat_w = qk_weight.reshape(width, 2 * cols)
    partial_value = jnp.dot(normed_rows, flat_w, preferred_element_type=jnp.float32)
    flat_grads = norm_grads.reshape(tokens, 2 * cols)
    raw = lax.psum(partial_value.astype(jnp.bfloat16), "mx").astype(jnp.float32)
    d_raw = head_norm_back(raw, flat_grads)
    local_token_rows = tokens // lax.axis_size("my")
    left = d_raw
    normed_gradient = lax.psum_scatter(
        lax.dot_general(
            left, flat_w, (((1,), (1,)), ((), ())), preferred_element_type=jnp.float32
        ).astype(jnp.bfloat16),
        "my",
        scatter_dimension=0,
        tiled=True,
    ).astype(jnp.float32)
    row_offset = lax.axis_index("my") * local_token_rows
    local_input = lax.dynamic_slice_in_dim(saved_block_input, row_offset, local_token_rows, 0)
    local_means = lax.dynamic_slice_in_dim(token_row_mean, row_offset, local_token_rows, 0)
    local_centred = local_input.astype(jnp.float32) - local_means[:, None]
    sum_one, sum_two = lax.psum(
        (jnp.sum(normed_gradient, axis=1), jnp.sum(normed_gradient * local_centred, axis=1)), "mx"
    )
    first_mean_term = (sum_one / D)[:, None]
    second_mean_term = (sum_two / D)[:, None]
    block_input_gradient = (
        normed_gradient - first_mean_term - local_centred * second_mean_term
    ).astype(jnp.bfloat16)
    left = normed_rows
    weight_sum = lax.psum_scatter(
        lax.dot_general(
            left, d_raw, (((0,), (0,)), ((), ())), preferred_element_type=jnp.float32
        ).astype(jnp.bfloat16),
        "dp",
        scatter_dimension=0,
        tiled=True,
    ).astype(jnp.float32)
    weight_grad = weight_sum.reshape(weight_sum.shape[0], 2, cols)
    return (block_input_gradient, weight_grad)


def solution(mesh):
    return jax.shard_map(
        per_device,
        mesh=mesh,
        in_specs=(P("dp", "mx"), P("dp"), P("mx", None, "my"), P("dp", None, "my")),
        out_specs=(P(("dp", "my"), "mx"), P(("mx", "dp"), None, "my")),
        check_vma=False,
    )
```

profile of v0, /device:TPU:1, one launch (start us, length us, event | category | flops | bytes accessed | tf_op | source)
XLA Modules:
  0.0 381.2 jit_solution(873572314231615566)
XLA Ops:
  7.2 2.2 copy.15
  9.5 1.4 copy-done
  10.9 1.6 convolution_convert_fusion.2
  12.5 0.5 copy.7
  13.1 0.3 copy.14
  13.4 84.0 %all-reduce.3.cloned.1.call-done = bf16[256,768]{1,0:T(8,128)(2,1)} async-done(((bf16[256,768]{1,0:T(8,128)(2,1)}), bf16[256,768]{1,0:T(8,128)(2,1)}) %all-reduce.3.cloned.1.call-update) | async-done | bytes 393232 | tf_op jit(solution)/shard_map/psum | solution.py:32
  97.4 1.2 copy.6
  98.7 0.2 fusion.3
  99.0 0.3 copy.12
  99.3 0.3 copy.9
  99.6 1.0 mul.48
  100.6 1.4 copy.13
  102.0 0.9 sub.61
  102.9 2.3 copy.10
  105.2 1.6 multiply_convert_fusion
  106.8 0.7 copy-done.3
  107.5 1.7 convolution_convert_fusion.1
  109.3 3.3 convolution_convert_fusion
  112.7 70.3 %reduce-scatter.3.cloned.1.call-done = bf16[32,1536]{1,0:T(8,128)(2,1)} async-done(((bf16[256,1536]{1,0:T(8,128)(2,1)}), bf16[32,1536]{1,0:T(8,128)(2,1)}) %reduce-scatter.3.cloned.1.call-update) | async-done | bytes 98320 | tf_op jit(solution)/shard_map/reduce_scatter | solution.py:36
  183.0 1.1 convert_reduce_fusion
  184.1 8.1 %all-reduce = (f32[32]{0:T(128)S(1)}, f32[32]{0:T(128)S(1)}) all-reduce(f32[32]{0:T(128)S(1)} %get-tuple-element.5, f32[32]{0:T(128)S(1)} %get-tuple-element.4), channel_id=1, replica_groups=mesh['dp'=32,'mx'=4,'my'=8] {'mx'}, use_global_device_ids=true, to_apply=%region_9.0 | all-reduce | flops 64 | bytes 512 | tf_op jit(solution)/shard_map/psum | solution.py:48
  192.3 1.6 fusion.1
  193.9 179.2 %reduce-scatter.5.cloned.1.call-done = bf16[48,768]{1,0:T(8,128)(2,1)} async-done(((bf16[1536,768]{1,0:T(8,128)(2,1)}), bf16[48,768]{1,0:T(8,128)(2,1)}) %reduce-scatter.5.cloned.1.call-update) | async-done | bytes 73744 | tf_op jit(solution)/shard_map/reduce_scatter | solution.py:57
  373.1 1.6 reshape.61
  (33 shorter events, 0.7 us)
Async XLA Ops:
  7.2 90.2 %all-reduce.3.cloned.1.call-start = ((), (), s32[]{:S(2)}) async-start(), calls=%async_computation.2 | async-start | bytes 786432 | tf_op jit(solution)/shard_map/psum | solution.py:32
  7.2 3.6 copy-start.4
  7.2 3.6 copy-start.7
  9.4 1.4 copy-start
  10.9 1.7 copy-start.6
  12.5 170.6 %reduce-scatter.3.cloned.1.call-start = ((), (), s32[]{:S(2)}) async-start(), calls=%async_computation.3 | async-start | bytes 884736 | tf_op jit(solution)/shard_map/reduce_scatter | solution.py:36
  99.6 5.6 %copy-start.2 = (bf16[256,768]{1,0:T(8,128)(2,1)S(1)}, bf16[256,768]{1,0:T(8,128)(2,1)}, u32[]{:S(2)}) copy-start(bf16[256,768]{1,0:T(8,128)(2,1)} %all-reduce.3.cloned.1.call-done) | copy-start | bytes 1179652
  105.2 2.3 copy-start.1
  106.7 0.7 copy-start.3
  107.5 1.8 copy-start.5
  107.5 1.8 copy-start.8
  109.2 263.8 %reduce-scatter.5.cloned.1.call-start = ((), (), s32[]{:S(2)}) async-start(), calls=%async_computation.4 | async-start | bytes 2433024 | tf_op jit(solution)/shard_map/reduce_scatter | solution.py:57
Sparse Core Ops, SparseCore 0:
  12.6 84.7 all-reduce.2
  109.4 73.6 reduce-scatter.2
  188.7 184.3 reduce-scatter.4
where the time goes:
time: 382 us; the launch traced here: 381 us
  waiting for transfers between devices  334 us (87%)
  local copies, waits for them, and re-layouts  14.2 us (4%)
  between operations  13.9 us (4%)
  blocking collectives  8.11 us (2%)
  matrix products  6.62 us (2%)
  other arithmetic  4.71 us (1%)
    reduce_scatter x1, waiting for transfers between devices, per_device(): lax.psum_scatter(lax.dot_general(left, d_raw, (((0,), (0,)), ((), ())), p...  179 us
    psum x1, waiting for transfers between devices, per_device(): raw = lax.psum(partial_value.astype(jnp.bfloat16), 'mx').astype(jnp.float32)  84 us
    reduce_scatter x1, waiting for transfers between devices, per_device(): lax.psum_scatter(lax.dot_general(left, flat_w, (((1,), (1,)), ((), ())),...  70.3 us
    psum x1, blocking collectives, per_device(): lax.psum((jnp.sum(normed_gradient, axis=1), jnp.sum(normed_gradient * loc...  8.11 us
  transfers between devices with their start and end apart: 3, of which 3 were waited for; matrix products, arithmetic and copies ran while one was open for 2% of the time, Pallas kernels for 0%

commit v1 on v0

v1 whole, which is shorter than its diff:
```python
import functools

import jax
import jax.numpy as jnp
from jax import lax
from jax.experimental import pallas as pl
from jax.experimental.pallas import tpu as pltpu
from jax.sharding import Mesh, PartitionSpec as P

D = 6144
HEAD_DIM = 128
CHUNKS = (0, 4, 2, 6, 1, 5, 3, 7)
TOK = 256
CHUNK = 32
EXTRA = 16
BLOCK = 48


def chunk_rows(k):
    place = lax.axis_index("my")
    return pl.ds(pl.multiple_of(lax.bitwise_xor(place, k) * CHUNK, CHUNK), CHUNK)


def pairings(z, c):
    near, wrap = lax.bitwise_xor(z, 1), 3 - z
    first = jnp.where(c == 0, near, wrap)
    second = jnp.where(c == 0, wrap, near)
    return first, second


def project_kernel(x_ref, mean_ref, w_ref, send_ref, own_ref, other_ref, normed, turned):
    for place, k in enumerate(CHUNKS):
        rows = chunk_rows(k)
        centred = x_ref[rows, :].astype(jnp.float32) - mean_ref[rows, :]
        normed[place * CHUNK : (place + 1) * CHUNK, :] = centred.astype(jnp.bfloat16)
    w = w_ref[...]
    part = jnp.dot(normed[...], w, preferred_element_type=jnp.float32).astype(jnp.bfloat16)
    ones = jnp.ones((EXTRA, w.shape[0]), jnp.bfloat16)
    sums = jnp.dot(ones, w, preferred_element_type=jnp.float32)
    high = sums.astype(jnp.bfloat16).astype(jnp.float32)
    row = lax.broadcasted_iota(jnp.int32, sums.shape, 0)
    extra = jnp.where(row == 0, high, jnp.where(row == 1, sums - high, 0.0)).astype(jnp.bfloat16)
    for q in range(send_ref.shape[0]):
        send_ref[q, :TOK, :] = part
        send_ref[q, TOK:, :] = extra
    turned[...] = normed[...].T
    z, c = lax.axis_index("zh"), lax.axis_index("c")
    for mine, out in ((True, own_ref), (False, other_ref)):
        core = c if mine else 1 - c
        first, second = pairings(z, core)
        for x in range(4):
            for place, target in enumerate((z, second, first, lax.bitwise_xor(z, 2))):
                row0 = pl.multiple_of(((x * 4 + target) * 2 + core) * BLOCK, BLOCK)
                at = (x * 4 + place) * BLOCK
                out[at : at + BLOCK, :] = turned[pl.ds(row0, BLOCK), :]


def norm_kernel(parts_ref, g_ref, d_ref, stat_ref, g_scr):
    for place, k in enumerate(CHUNKS):
        g_scr[place * CHUNK : (place + 1) * CHUNK, :] = g_ref[chunk_rows(k), :].astype(jnp.float32)
    n = parts_ref.shape[0]
    one = jnp.zeros((TOK, 1), jnp.float32)
    two = jnp.zeros((TOK, 1), jnp.float32)
    for h in range(d_ref.shape[1] // HEAD_DIM):
        cols = slice(h * HEAD_DIM, (h + 1) * HEAD_DIM)
        raw = sum(parts_ref[q, :TOK, cols].astype(jnp.float32) for q in range(n))
        tail = sum(parts_ref[q, TOK:, cols].astype(jnp.float32) for q in range(n))
        column_sums = jnp.sum(tail, axis=0, keepdims=True)
        g = g_scr[:, cols]
        off = raw - jnp.mean(raw, axis=1, keepdims=True)
        rs = lax.rsqrt(jnp.mean(off * off, axis=1, keepdims=True) + 1e-06)
        z = off * rs
        d = rs * (g - jnp.mean(g, axis=1, keepdims=True) - z * jnp.mean(g * z, axis=1, keepdims=True))
        d = d.astype(jnp.bfloat16)
        d_ref[:, cols] = d
        wide = d.astype(jnp.float32)
        one += jnp.sum(wide * column_sums, axis=1, keepdims=True)
        two += jnp.sum(wide * raw, axis=1, keepdims=True)
    lane = lax.broadcasted_iota(jnp.int32, stat_ref.shape, 1)
    stat_ref[...] = jnp.where(lane == 0, one, two) * (1.0 / D)


def input_grad_kernel(d_ref, w_ref, stat_ref, x_ref, mean_ref, keep_ref, send_ref):
    half = keep_ref.shape[0]
    for out, first in ((send_ref, 4), (keep_ref, 0)):
        at = first * CHUNK
        part = lax.dot_general(
            d_ref[at : at + half, :], w_ref[...], (((1,), (1,)), ((), ())), preferred_element_type=jnp.float32
        )
        for i in range(4):
            rows = chunk_rows(CHUNKS[first + i])
            here = slice(at + i * CHUNK, at + (i + 1) * CHUNK)
            centred = x_ref[rows, :].astype(jnp.float32) - mean_ref[rows, :]
            value = part[i * CHUNK : (i + 1) * CHUNK, :] - stat_ref[here, 0:1] - centred * stat_ref[here, 1:2]
            out[i * CHUNK : (i + 1) * CHUNK, :] = value.astype(jnp.bfloat16)


def weight_grad_kernel(own_ref, other_ref, d_ref, d_other_ref, out_ref):
    rows = out_ref.shape[1]
    for q in range(out_ref.shape[0]):
        at = slice(q * rows, (q + 1) * rows)
        total = jnp.dot(own_ref[at, :], d_ref[...], preferred_element_type=jnp.float32)
        total += jnp.dot(other_ref[at, :], d_other_ref[...], preferred_element_type=jnp.float32)
        out_ref[q] = total.astype(jnp.bfloat16)


def call(kernel, outs, flops, scratch=()):
    return pl.pallas_call(
        kernel,
        out_shape=[jax.ShapeDtypeStruct(s, t) for s, t in outs],
        scratch_shapes=[pltpu.VMEM(s, t) for s, t in scratch],
        compiler_params=pltpu.CompilerParams(vmem_limit_bytes=40 * 1024 * 1024),
        cost_estimate=pl.CostEstimate(flops=flops, bytes_accessed=4 * 1024 * 1024, transcendentals=0),
    )


def per_device(x, mean, weight, grads):
    bf, f32 = jnp.bfloat16, jnp.float32
    tokens, width = x.shape
    cols = 2 * weight.shape[2]
    w = weight.reshape(width, cols)
    g = grads.reshape(tokens, cols)
    mean = mean.reshape(tokens, 1)
    half = width // 2
    work = 2 * tokens * width * cols
    send, own, other = call(
        project_kernel,
        [((4, tokens + EXTRA, cols), bf), ((half, tokens), bf), ((half, tokens), bf)],
        work,
        [((tokens, width), bf), ((width, tokens), bf)],
    )(x, mean, w)
    core_swap = [(0, 1), (1, 0)]
    other = lax.ppermute(other, "c", core_swap)
    parts = lax.all_to_all(send, "mx", 0, 0)
    d_raw, stat = call(
        norm_kernel, [((tokens, cols), bf), ((tokens, 128), f32)], 40 * tokens * cols, [((tokens, cols), f32)]
    )(parts, g)
    d_other = lax.ppermute(d_raw, "c", core_swap)
    keep, away = call(input_grad_kernel, [((tokens // 2, width), bf)] * 2, work)(d_raw, w, stat, x, mean)
    (dw,) = call(weight_grad_kernel, [((4, half // 4, cols), bf)], work)(own, other, d_raw, d_other)

    for bit in (1, 2, 4):
        got = lax.ppermute(away, "my", [(i, i ^ bit) for i in range(8)])
        total = keep.astype(f32) + got.astype(f32)
        n = total.shape[0] // 2
        if bit < 4:
            keep, away = total[:n], total[n:].astype(bf)
    input_grad = total.astype(bf)

    got = lax.all_to_all(dw, "x", 0, 0)
    total = jnp.sum(got.astype(f32), axis=0)
    for step in range(2):
        n = total.shape[0] // 2
        keep, away = total[:n], total[n:].astype(bf)
        pairs = []
        for z in range(4):
            for c in range(2):
                partner = (z ^ 1) if step == c else 3 - z
                pairs.append((2 * z + c, 2 * partner + c))
        got = lax.ppermute(away, ("zh", "c"), pairs)
        total = keep + got.astype(f32)
    return input_grad, total.reshape(BLOCK, 2, cols // 2)


def solution(mesh):
    fine = Mesh(mesh.devices.reshape(4, 4, 2, 4, 8), ("x", "zh", "c", "mx", "my"))
    dp = ("x", "zh", "c")
    return jax.shard_map(
        per_device,
        mesh=fine,
        in_specs=(P(dp, "mx"), P(dp), P("mx", None, "my"), P(dp, None, "my")),
        out_specs=(P((*dp, "my"), "mx"), P(("mx", *dp), None, "my")),
        check_vma=False,
    )
```

time: 382 us -> 127 us (0.33)
  the two profiles are of different devices: /device:TPU:1 before, /device:TPU:96 now
where the time goes in v1:
time: 127 us; the launch traced here: 126 us
  starting transfers between devices  63.6 us (50%)
  waiting for transfers between devices  44 us (35%)
  Pallas kernels  9.64 us (8%)
  local copies, waits for them, and re-layouts  6.91 us (5%)
    ppermute x2, starting transfers between devices, per_device(): got = lax.ppermute(away, ('zh', 'c'), pairs)  35.2 us
    all_to_all x1, waiting for transfers between devices, per_device(): parts = lax.all_to_all(send, 'mx', 0, 0)  19.1 us
    ppermute x3, starting transfers between devices, per_device(): got = lax.ppermute(away, 'my', [(i, i ^ bit) for i in range(8)])  15.9 us
    ppermute x2, waiting for transfers between devices, per_device(): got = lax.ppermute(away, ('zh', 'c'), pairs)  12.7 us
    all_to_all x1, waiting for transfers between devices, per_device(): got = lax.all_to_all(dw, 'x', 0, 0)  7.74 us
    unnamed x18, local copies, waits for them, and re-layouts  5.97 us
    all_to_all x1, starting transfers between devices, per_device(): parts = lax.all_to_all(send, 'mx', 0, 0)  4.46 us
    ppermute x3, waiting for transfers between devices, per_device(): got = lax.ppermute(away, 'my', [(i, i ^ bit) for i in range(8)])  4.44 us
  transfers between devices with their start and end apart: 9, of which 5 were waited for; matrix products, arithmetic and copies ran while one was open for 2% of the time, Pallas kernels for 7%

profile of v1, /device:TPU:96, one launch (start us, length us, event | category | flops | bytes accessed | tf_op | source)
XLA Modules:
  0.0 126.0 jit_solution(12987937150775199927)
XLA Ops:
  0.6 2.2 %copy.8 = bf16[192,8,2,384]{3,1,2,0:T(8,128)(2,1)S(1)} copy(bf16[192,8,2,384]{3,2,1,0:T(2,128)(2,1)} %bitcast.8) | data formatting | bytes 4718592
  3.0 1.2 shard_map.59
  4.2 1.2 copy-done.1
  5.4 0.7 copy-done.4
  6.2 0.8 copy-done.6
  6.9 4.5 %all-to-all-start = ((bf16[4,272,768]{2,1,0:T(8,128)(2,1)}), bf16[4,272,768]{2,1,0:T(8,128)(2,1)}, u32[]{:S(2)}, u32[]{:S(2)}) async-start(bf16[4,272,768]{2,1,0:T(8,128)(2,1)} %copy-done.1), calls=%async_computation | async-start | bytes 3342336 | tf_op jit(solution)/shard_map/all_to_all | solution.py:134
  11.4 1.9 %collective-permute-start.3 = (bf16[768,256]{1,0:T(8,128)(2,1)}, bf16[768,256]{1,0:T(8,128)(2,1)}, u32[]{:S(2)}, u32[]{:S(2)}) collective-permute-start(bf16[768,256]{1,0:T(8,128)(2,1)} %copy-done.6), channel_id=1, source_target_pairs={{0,32},{32,0},{1,33},{33,1},{2,34},{34,2},{3,35},{35,3},{4,36},{36... | collective-permute-start | bytes 1179656 | tf_op jit(solution)/shard_map/ppermute | solution.py:133
  13.3 1.0 copy.9
  14.4 19.1 %all-to-all-done.parts_ref = bf16[4,272,768]{2,1,0:T(8,128)(2,1)} async-done(((bf16[4,272,768]{2,1,0:T(8,128)(2,1)}), bf16[4,272,768]{2,1,0:T(8,128)(2,1)}, u32[]{:S(2)}, u32[]{:S(2)}) %all-to-all-start) | async-done | bytes 1671200 | tf_op jit(solution)/shard_map/all_to_all | solution.py:134
  33.4 3.4 %shard_map.60 = (bf16[256,768]{1,0:T(8,128)(2,1)S(1)}, f32[256,128]{1,0:T(8,128)S(1)}) custom-call(bf16[4,272,768]{2,1,0:T(8,128)(2,1)} %all-to-all-done.parts_ref, bf16[256,768]{1,0:T(8,128)(2,1)S(1)} %bitcast.7), custom_call_target="tpu_custom_call" | custom-call | flops 7864320 | bytes 4194304 | tf_op jit(solution)/shard_map/pallas_call | solution.py:135
  36.8 1.9 %collective-permute-start.4 = (bf16[256,768]{1,0:T(8,128)(2,1)S(1)}, bf16[256,768]{1,0:T(8,128)(2,1)S(1)}, u32[]{:S(2)}, u32[]{:S(2)}) collective-permute-start(bf16[256,768]{1,0:T(8,128)(2,1)S(1)} %get-tuple-element.10.d_ref), channel_id=1, source_target_pairs={{0,32},{32,0},{1,33},{33,1},{2,34},{34,2},{3,35},{35,3},{4,36},{36... | collective-permute-start | bytes 1179656 | tf_op jit(solution)/shard_map/ppermute | solution.py:138
  38.8 2.2 %shard_map.61 = (bf16[128,1536]{1,0:T(8,128)(2,1)S(1)}, bf16[128,1536]{1,0:T(8,128)(2,1)}) custom-call(bf16[256,768]{1,0:T(8,128)(2,1)S(1)} %get-tuple-element.10.d_ref, bf16[1536,768]{1,0:T(8,128)(2,1)S(1)} %bitcast.6, f32[256,128]{1,0:T(8,128)S(1)} %get-tuple-element.11.stat_ref, bf16[256,1536]{1,0:T(8,128)(2,1)S(1)} %copy-done, f32[256,1]{1,0:T(8,128)S(1)} %copy-done.3), custom_call_target="tpu_custom_call" | custom-call | flops 603979776 | bytes 4194304 | tf_op jit(solution)/shard_map/pallas_call | solution.py:139
  41.0 2.0 %collective-permute-start = (bf16[128,1536]{1,0:T(8,128)(2,1)}, bf16[128,1536]{1,0:T(8,128)(2,1)S(1)}, u32[]{:S(2)}, u32[]{:S(2)}) collective-permute-start(bf16[128,1536]{1,0:T(8,128)(2,1)} %get-tuple-element.13), channel_id=1, source_target_pairs={{0,1},{1,0},{2,3},{3,2},{4,5},{5,4},{6,7},{7,6},{8,9},{9,8},{10,11... | collective-permute-start | bytes 1179656 | tf_op jit(solution)/shard_map/ppermute | solution.py:143
  43.0 2.8 %shard_map.62 = bf16[4,192,768]{2,1,0:T(8,128)(2,1)} custom-call(bf16[768,256]{1,0:T(8,128)(2,1)S(1)} %copy-done.5, bf16[768,256]{1,0:T(8,128)(2,1)} %collective-permute-done.3.other_ref, bf16[256,768]{1,0:T(8,128)(2,1)S(1)} %get-tuple-element.10.d_ref, bf16[256,768]{1,0:T(8,128)(2,1)S(1)} %collective-permute-done.4.d_other_ref), custom_call_target="tpu_custom_call" | custom-call | flops 603979776 | bytes 4194304 | tf_op jit(solution)/shard_map/pallas_call | solution.py:140
  45.9 4.3 %all-to-all-start.1 = ((bf16[4,192,768]{2,1,0:T(8,128)(2,1)}), bf16[4,192,768]{2,1,0:T(8,128)(2,1)S(1)}, u32[]{:S(2)}, u32[]{:S(2)}) async-start(bf16[4,192,768]{2,1,0:T(8,128)(2,1)} %shard_map.62), calls=%async_computation.1 | async-start | bytes 2359296 | tf_op jit(solution)/shard_map/all_to_all | solution.py:150
  50.2 4.4 %collective-permute-done = bf16[128,1536]{1,0:T(8,128)(2,1)S(1)} collective-permute-done((bf16[128,1536]{1,0:T(8,128)(2,1)}, bf16[128,1536]{1,0:T(8,128)(2,1)S(1)}, u32[]{:S(2)}, u32[]{:S(2)}) %collective-permute-start) | collective-permute-done | bytes 393248 | tf_op jit(solution)/shard_map/ppermute | solution.py:143
  54.7 4.8 %collective-permute-start.1 = (bf16[64,1536]{1,0:T(8,128)(2,1)S(1)}, bf16[64,1536]{1,0:T(8,128)(2,1)S(1)}, u32[]{:S(2)}, u32[]{:S(2)}) collective-permute-start(bf16[64,1536]{1,0:T(8,128)(2,1)S(1)} %slice.54), channel_id=1, source_target_pairs={{0,2},{1,3},{2,0},{3,1},{4,6},{5,7},{6,4},{7,5},{8,10},{9,11},{10,... | collective-permute-start | bytes 589832 | tf_op jit(solution)/shard_map/ppermute | solution.py:143
  59.5 7.7 %all-to-all-done.1 = bf16[4,192,768]{2,1,0:T(8,128)(2,1)S(1)} async-done(((bf16[4,192,768]{2,1,0:T(8,128)(2,1)}), bf16[4,192,768]{2,1,0:T(8,128)(2,1)S(1)}, u32[]{:S(2)}, u32[]{:S(2)}) %all-to-all-start.1) | async-done | bytes 1179680 | tf_op jit(solution)/shard_map/all_to_all | solution.py:150
  67.4 15.7 %collective-permute-start.5 = (bf16[96,768]{1,0:T(8,128)(2,1)S(1)}, bf16[96,768]{1,0:T(8,128)(2,1)S(1)}, u32[]{:S(2)}, u32[]{:S(2)}) collective-permute-start(bf16[96,768]{1,0:T(8,128)(2,1)S(1)} %slice.55), channel_id=1, source_target_pairs={{0,64},{32,224},{64,0},{96,160},{128,192},{160,96},{192,128},{224,... | collective-permute-start | bytes 442376 | tf_op jit(solution)/shard_map/ppermute | solution.py:160
  83.3 9.1 %collective-permute-start.2 = (bf16[32,1536]{1,0:T(8,128)(2,1)S(1)}, bf16[32,1536]{1,0:T(8,128)(2,1)S(1)}, u32[]{:S(2)}, u32[]{:S(2)}) collective-permute-start(bf16[32,1536]{1,0:T(8,128)(2,1)S(1)} %slice.56), channel_id=1, source_target_pairs={{0,4},{1,5},{2,6},{3,7},{4,0},{5,1},{6,2},{7,3},{8,12},{9,13},{10,... | collective-permute-start | bytes 294920 | tf_op jit(solution)/shard_map/ppermute | solution.py:143
  92.4 10.7 %collective-permute-done.5 = bf16[96,768]{1,0:T(8,128)(2,1)S(1)} collective-permute-done((bf16[96,768]{1,0:T(8,128)(2,1)S(1)}, bf16[96,768]{1,0:T(8,128)(2,1)S(1)}, u32[]{:S(2)}, u32[]{:S(2)}) %collective-permute-start.5) | collective-permute-done | bytes 147488 | tf_op jit(solution)/shard_map/ppermute | solution.py:160
  103.1 19.4 %collective-permute-start.6 = (bf16[48,768]{1,0:T(8,128)(2,1)S(1)}, bf16[48,768]{1,0:T(8,128)(2,1)S(1)}, u32[]{:S(2)}, u32[]{:S(2)}) collective-permute-start(bf16[48,768]{1,0:T(8,128)(2,1)S(1)} %slice.57), channel_id=1, source_target_pairs={{0,192},{32,96},{64,128},{96,32},{128,64},{160,224},{192,0},{224,1... | collective-permute-start | bytes 221192 | tf_op jit(solution)/shard_map/ppermute | solution.py:160
  123.3 2.0 %collective-permute-done.6 = bf16[48,768]{1,0:T(8,128)(2,1)S(1)} collective-permute-done((bf16[48,768]{1,0:T(8,128)(2,1)S(1)}, bf16[48,768]{1,0:T(8,128)(2,1)S(1)}, u32[]{:S(2)}, u32[]{:S(2)}) %collective-permute-start.6) | collective-permute-done | bytes 73760 | tf_op jit(solution)/shard_map/ppermute | solution.py:160
  125.3 0.7 reshape.19
  (28 shorter events, 1.2 us)
Async XLA Ops:
  0.6 2.2 %copy-start.7 = (f32[256]{0:T(256)S(1)}, f32[256]{0:T(256)}, u32[]{:S(2)}) copy-start(f32[256]{0:T(256)} %param.5) | copy-start | bytes 3076
  0.6 2.4 %copy-start = (bf16[256,1536]{1,0:T(8,128)(2,1)S(1)}, bf16[256,1536]{1,0:T(8,128)(2,1)}, u32[]{:S(2)}) copy-start(bf16[256,1536]{1,0:T(8,128)(2,1)} %x_ref.3) | copy-start | bytes 2359300
  3.0 3.9 %copy-start.2 = (f32[256,1]{1,0:T(8,128)}, f32[256,1]{1,0:T(8,128)S(1)}, u32[]{:S(2)}) copy-start(f32[256,1]{1,0:T(8,128)S(1)} %copy.6.mean_ref) | copy-start | bytes 3076
  4.2 1.2 copy-start.1
  5.4 0.7 copy-start.4
  6.2 0.8 copy-start.6
  6.9 26.5 %all-to-all-start = ((bf16[4,272,768]{2,1,0:T(8,128)(2,1)}), bf16[4,272,768]{2,1,0:T(8,128)(2,1)}, u32[]{:S(2)}, u32[]{:S(2)}) async-start(bf16[4,272,768]{2,1,0:T(8,128)(2,1)} %copy-done.1), calls=%async_computation | async-start | bytes 3342336 | tf_op jit(solution)/shard_map/all_to_all | solution.py:134
  11.4 31.6 %collective-permute-start.3 = (bf16[768,256]{1,0:T(8,128)(2,1)}, bf16[768,256]{1,0:T(8,128)(2,1)}, u32[]{:S(2)}, u32[]{:S(2)}) collective-permute-start(bf16[768,256]{1,0:T(8,128)(2,1)} %copy-done.6), channel_id=1, source_target_pairs={{0,32},{32,0},{1,33},{33,1},{2,34},{34,2},{3,35},{35,3},{4,36},{36... | collective-permute-start | bytes 1179656 | tf_op jit(solution)/shard_map/ppermute | solution.py:133
  33.4 5.3 %copy-start.3 = (f32[256,1]{1,0:T(8,128)S(1)}, f32[256,1]{1,0:T(8,128)}, u32[]{:S(2)}) copy-start(f32[256,1]{1,0:T(8,128)} %copy-done.2) | copy-start | bytes 3076
  36.8 6.2 %collective-permute-start.4 = (bf16[256,768]{1,0:T(8,128)(2,1)S(1)}, bf16[256,768]{1,0:T(8,128)(2,1)S(1)}, u32[]{:S(2)}, u32[]{:S(2)}) collective-permute-start(bf16[256,768]{1,0:T(8,128)(2,1)S(1)} %get-tuple-element.10.d_ref), channel_id=1, source_target_pairs={{0,32},{32,0},{1,33},{33,1},{2,34},{34,2},{3,35},{35,3},{4,36},{36... | collective-permute-start | bytes 1179656 | tf_op jit(solution)/shard_map/ppermute | solution.py:138
  38.8 4.3 %copy-start.5 = (bf16[768,256]{1,0:T(8,128)(2,1)S(1)}, bf16[768,256]{1,0:T(8,128)(2,1)}, u32[]{:S(2)}) copy-start(bf16[768,256]{1,0:T(8,128)(2,1)} %copy-done.4) | copy-start | bytes 1179652
  41.0 13.6 %collective-permute-start = (bf16[128,1536]{1,0:T(8,128)(2,1)}, bf16[128,1536]{1,0:T(8,128)(2,1)S(1)}, u32[]{:S(2)}, u32[]{:S(2)}) collective-permute-start(bf16[128,1536]{1,0:T(8,128)(2,1)} %get-tuple-element.13), channel_id=1, source_target_pairs={{0,1},{1,0},{2,3},{3,2},{4,5},{5,4},{6,7},{7,6},{8,9},{9,8},{10,11... | collective-permute-start | bytes 1179656 | tf_op jit(solution)/shard_map/ppermute | solution.py:143
  45.9 21.4 %all-to-all-start.1 = ((bf16[4,192,768]{2,1,0:T(8,128)(2,1)}), bf16[4,192,768]{2,1,0:T(8,128)(2,1)S(1)}, u32[]{:S(2)}, u32[]{:S(2)}) async-start(bf16[4,192,768]{2,1,0:T(8,128)(2,1)} %shard_map.62), calls=%async_computation.1 | async-start | bytes 2359296 | tf_op jit(solution)/shard_map/all_to_all | solution.py:150
  54.7 28.5 %collective-permute-start.1 = (bf16[64,1536]{1,0:T(8,128)(2,1)S(1)}, bf16[64,1536]{1,0:T(8,128)(2,1)S(1)}, u32[]{:S(2)}, u32[]{:S(2)}) collective-permute-start(bf16[64,1536]{1,0:T(8,128)(2,1)S(1)} %slice.54), channel_id=1, source_target_pairs={{0,2},{1,3},{2,0},{3,1},{4,6},{5,7},{6,4},{7,5},{8,10},{9,11},{10,... | collective-permute-start | bytes 589832 | tf_op jit(solution)/shard_map/ppermute | solution.py:143
  67.4 35.6 %collective-permute-start.5 = (bf16[96,768]{1,0:T(8,128)(2,1)S(1)}, bf16[96,768]{1,0:T(8,128)(2,1)S(1)}, u32[]{:S(2)}, u32[]{:S(2)}) collective-permute-start(bf16[96,768]{1,0:T(8,128)(2,1)S(1)} %slice.55), channel_id=1, source_target_pairs={{0,64},{32,224},{64,0},{96,160},{128,192},{160,96},{192,128},{224,... | collective-permute-start | bytes 442376 | tf_op jit(solution)/shard_map/ppermute | solution.py:160
  83.3 39.3 %collective-permute-start.2 = (bf16[32,1536]{1,0:T(8,128)(2,1)S(1)}, bf16[32,1536]{1,0:T(8,128)(2,1)S(1)}, u32[]{:S(2)}, u32[]{:S(2)}) collective-permute-start(bf16[32,1536]{1,0:T(8,128)(2,1)S(1)} %slice.56), channel_id=1, source_target_pairs={{0,4},{1,5},{2,6},{3,7},{4,0},{5,1},{6,2},{7,3},{8,12},{9,13},{10,... | collective-permute-start | bytes 294920 | tf_op jit(solution)/shard_map/ppermute | solution.py:143
  103.1 22.1 %collective-permute-start.6 = (bf16[48,768]{1,0:T(8,128)(2,1)S(1)}, bf16[48,768]{1,0:T(8,128)(2,1)S(1)}, u32[]{:S(2)}, u32[]{:S(2)}) collective-permute-start(bf16[48,768]{1,0:T(8,128)(2,1)S(1)} %slice.57), channel_id=1, source_target_pairs={{0,192},{32,96},{64,128},{96,32},{128,64},{160,224},{192,0},{224,1... | collective-permute-start | bytes 221192 | tf_op jit(solution)/shard_map/ppermute | solution.py:160

commit v2 on v1

v2 whole, which is shorter than its diff:
```python
import functools

import jax
import jax.numpy as jnp
from jax import lax
from jax.experimental import pallas as pl
from jax.experimental.pallas import tpu as pltpu
from jax.sharding import Mesh, PartitionSpec as P

D = 6144
HEAD_DIM = 128
CHUNKS = (0, 4, 2, 6, 1, 5, 3, 7)
CHUNK = 32
EXTRA = 16
QUARTER = 64
VMEM = 40 * 1024 * 1024
BLOCK = 48


def chunk_rows(k):
    place = lax.axis_index("my")
    return pl.ds(pl.multiple_of(lax.bitwise_xor(place, k) * CHUNK, CHUNK), CHUNK)


def pairings(z, c):
    near, wrap = lax.bitwise_xor(z, 1), 3 - z
    first = jnp.where(c == 0, near, wrap)
    second = jnp.where(c == 0, wrap, near)
    return first, second


def centre(x_ref, mean_ref, normed):
    by_row = [jnp.broadcast_to(mean_ref[i : i + 1, :], (HEAD_DIM, HEAD_DIM)).T[:, :1] for i in range(2)]
    by_row = jnp.concatenate(by_row, axis=0)
    centred = (x_ref[...].astype(jnp.float32) - by_row).astype(jnp.bfloat16)
    normed[...] = centred


def gather_chunks(x_ref, mean_ref, plain, normed):
    centre(x_ref, mean_ref, plain)
    for place, k in enumerate(CHUNKS):
        normed[place * CHUNK : (place + 1) * CHUNK, :] = plain[chunk_rows(k), :]


def project_kernel(x_ref, mean_ref, w_ref, send_ref, extra_ref, normed, plain):
    gather_chunks(x_ref, mean_ref, plain, normed)
    w = w_ref[...]
    part = jnp.dot(normed[...], w, preferred_element_type=jnp.float32).astype(jnp.bfloat16)
    for q in range(send_ref.shape[0]):
        send_ref[q] = part[q * QUARTER : (q + 1) * QUARTER, :]
    ones = jnp.ones((EXTRA, w.shape[0]), jnp.bfloat16)
    sums = jnp.dot(ones, w, preferred_element_type=jnp.float32)
    high = sums.astype(jnp.bfloat16).astype(jnp.float32)
    row = lax.broadcasted_iota(jnp.int32, sums.shape, 0)
    extra = jnp.where(row == 0, high, jnp.where(row == 1, sums - high, 0.0))
    extra_ref[...] = extra.astype(jnp.bfloat16)


def norm_kernel(parts_ref, g_ref, extra_ref, out_ref):
    n = parts_ref.shape[0]
    y = lax.axis_index("mx")
    low = 2 * lax.rem(y, 2) + lax.div(y, 2)
    upper, lower = chunk_rows(low), chunk_rows(low + 4)
    two = jnp.zeros((QUARTER, HEAD_DIM), jnp.float32)
    for h in range(out_ref.shape[2] // HEAD_DIM):
        cols = slice(h * HEAD_DIM, (h + 1) * HEAD_DIM)
        raw = sum(parts_ref[q, :, cols].astype(jnp.float32) for q in range(n))
        g = jnp.concatenate([g_ref[upper, cols], g_ref[lower, cols]], axis=0).astype(jnp.float32)
        off = raw - jnp.mean(raw, axis=1, keepdims=True)
        rs = lax.rsqrt(jnp.mean(off * off, axis=1, keepdims=True) + 1e-06)
        z = off * rs
        d = rs * (g - jnp.mean(g, axis=1, keepdims=True) - z * jnp.mean(g * z, axis=1, keepdims=True))
        d = d.astype(jnp.bfloat16)
        for q in range(n):
            out_ref[q, :QUARTER, cols] = d
        two += d.astype(jnp.float32) * raw
    two = jnp.sum(two, axis=1, keepdims=True)
    high = two.astype(jnp.bfloat16).astype(jnp.float32)
    lane = lax.broadcasted_iota(jnp.int32, (QUARTER, HEAD_DIM), 1)
    stat = jnp.where(lane == 2, high, jnp.where(lane == 3, two - high, 0.0))
    stat = jnp.concatenate([stat, jnp.zeros_like(stat)], axis=0).T[:EXTRA, :].astype(jnp.bfloat16)
    for q in range(n):
        out_ref[q, QUARTER:, :HEAD_DIM] = extra_ref[:, :HEAD_DIM] + stat
        out_ref[q, QUARTER:, HEAD_DIM:] = extra_ref[:, HEAD_DIM:]


def input_grad_kernel(d_ref, w_ref, x_ref, mean_ref, keep_ref, send_ref, d_all, centred_all):
    n = d_ref.shape[0]
    by_row = [jnp.broadcast_to(mean_ref[i : i + 1, :], (HEAD_DIM, HEAD_DIM)).T[:, :1] for i in range(2)]
    centred_all[...] = x_ref[...].astype(jnp.float32) - jnp.concatenate(by_row, axis=0)
    for q in range(n):
        d_all[q * QUARTER : (q + 1) * QUARTER, :] = d_ref[q, :QUARTER, :]
    across = (((1,), (1,)), ((), ()))
    extra = jnp.concatenate([d_ref[q, QUARTER:, :] for q in range(n)], axis=0)
    one = lax.dot_general(d_all[...], extra, across, preferred_element_type=jnp.float32)
    lane = lax.broadcasted_iota(jnp.int32, one.shape, 1)
    one = jnp.sum(jnp.where(lax.rem(lane, EXTRA) < 2, one, 0.0), axis=1, keepdims=True) * (1.0 / D)
    two = [d_ref[q, QUARTER:, :HEAD_DIM].astype(jnp.float32).T[:QUARTER, :] for q in range(n)]
    two = jnp.concatenate([(t[:, 2:3] + t[:, 3:4]) * (1.0 / D) for t in two], axis=0)
    half = keep_ref.shape[0]
    for out, first in ((send_ref, 4), (keep_ref, 0)):
        at = first * CHUNK
        part = lax.dot_general(d_all[at : at + half, :], w_ref[...], across, preferred_element_type=jnp.float32)
        for i in range(4):
            rows = chunk_rows(CHUNKS[first + i])
            here = slice(at + i * CHUNK, at + (i + 1) * CHUNK)
            centred = centred_all[rows, :]
            value = part[i * CHUNK : (i + 1) * CHUNK, :] - one[here, :] - centred * two[here, :]
            out[i * CHUNK : (i + 1) * CHUNK, :] = value.astype(jnp.bfloat16)


def weight_grad_kernel(d_ref, x_ref, mean_ref, mine_ref, away_ref, d_all, normed, plain, total):
    for q in range(d_ref.shape[0]):
        d_all[q * QUARTER : (q + 1) * QUARTER, :] = d_ref[q, :QUARTER, :]
    gather_chunks(x_ref, mean_ref, plain, normed)
    total[...] = jnp.dot(normed[...].T, d_all[...], preferred_element_type=jnp.float32)
    z, c = lax.axis_index("zh"), lax.axis_index("c")
    for core, out in ((1 - c, away_ref), (c, mine_ref)):
        first, second = pairings(z, core)
        for x in range(4):
            for place, target in enumerate((z, second, first, lax.bitwise_xor(z, 2))):
                row0 = pl.multiple_of(((x * 4 + target) * 2 + core) * BLOCK, BLOCK)
                at = (x * 4 + place) * BLOCK
                out[at : at + BLOCK, :] = total[pl.ds(row0, BLOCK), :].astype(out.dtype)


def call(kernel, outs, flops, scratch=()):
    return pl.pallas_call(
        kernel,
        out_shape=[jax.ShapeDtypeStruct(s, t) for s, t in outs],
        scratch_shapes=[pltpu.VMEM(s, t) for s, t in scratch],
        compiler_params=pltpu.CompilerParams(vmem_limit_bytes=VMEM),
        cost_estimate=pl.CostEstimate(flops=flops, bytes_accessed=4 * 1024 * 1024, transcendentals=0),
    )


def per_device(x, mean, weight, grads):
    bf, f32 = jnp.bfloat16, jnp.float32
    tokens, width = x.shape
    cols = 2 * weight.shape[2]
    w = weight.reshape(width, cols)
    g = grads.reshape(tokens, cols)
    mean = mean.reshape(2, tokens // 2)
    half = width // 2
    work = 2 * tokens * width * cols
    whole = (tokens, width), bf
    send, extra = call(project_kernel, [((4, QUARTER, cols), bf), ((EXTRA, cols), bf)], work, [whole, whole])(x, mean, w)
    parts = lax.all_to_all(send, "mx", 0, 0)
    (d_mine,) = call(norm_kernel, [((4, QUARTER + EXTRA, cols), bf)], 10 * tokens * cols)(parts, g, extra)
    d = lax.all_to_all(d_mine, "mx", 0, 0)
    flat = (tokens, cols), bf
    mine, other = call(
        weight_grad_kernel, [((half, cols), bf)] * 2, work, [flat, whole, whole, ((width, cols), f32)]
    )(d, x, mean)
    got = lax.ppermute(other, "c", [(0, 1), (1, 0)])
    keep, away = call(
        input_grad_kernel, [((tokens // 2, width), bf)] * 2, work, [flat, ((tokens, width), f32)]
    )(d, w, x, mean)
    dw = (mine.astype(f32) + got.astype(f32)).astype(bf).reshape(4, half // 4, cols)

    for bit in (1, 2, 4):
        got = lax.ppermute(away, "my", [(i, i ^ bit) for i in range(8)])
        total = keep.astype(f32) + got.astype(f32)
        n = total.shape[0] // 2
        if bit < 4:
            keep, away = total[:n], total[n:].astype(bf)
    input_grad = total.astype(bf)

    got = lax.all_to_all(dw, "x", 0, 0)
    total = jnp.sum(got.astype(f32), axis=0)
    for step in range(2):
        n = total.shape[0] // 2
        keep, away = total[:n], total[n:].astype(bf)
        pairs = []
        for z in range(4):
            for c in range(2):
                partner = (z ^ 1) if step == c else 3 - z
                pairs.append((2 * z + c, 2 * partner + c))
        got = lax.ppermute(away, ("zh", "c"), pairs)
        total = keep + got.astype(f32)
    return input_grad, total.reshape(BLOCK, 2, cols // 2)


def solution(mesh):
    fine = Mesh(mesh.devices.reshape(4, 4, 2, 4, 8), ("x", "zh", "c", "mx", "my"))
    dp = ("x", "zh", "c")
    return jax.shard_map(
        per_device,
        mesh=fine,
        in_specs=(P(dp, "mx"), P(dp), P("mx", None, "my"), P(dp, None, "my")),
        out_specs=(P((*dp, "my"), "mx"), P(("mx", *dp), None, "my")),
        check_vma=False,
    )
```

time: 127 us -> 120 us (0.945)
  waiting for transfers between devices: 44 us -> 25.2 us
  blocking collectives: 0 us -> 10.3 us
  Pallas kernels: 9.64 us -> 5.07 us
  starting transfers between devices: 63.6 us -> 68.1 us
  other arithmetic: 1 us -> 2.31 us
    all_to_all x1, waiting for transfers between devices: 19.1 us -> 6.28 us  [per_device(): parts = lax.all_to_all(send, 'mx', 0, 0)]
    all_to_all x0 -> x1, blocking collectives: none -> 10.3 us  [per_device(): d = lax.all_to_all(d_mine, 'mx', 0, 0)]
    all_to_all x1, waiting for transfers between devices: 7.74 us -> 0.01 us  [per_device(): got = lax.all_to_all(dw, 'x', 0, 0)]
    ppermute x3, starting transfers between devices: 15.9 us -> 22.4 us  [per_device(): got = lax.ppermute(away, 'my', [(i, i ^ bit) for i in range(8)])]
    pallas_call x4, Pallas kernels: 9.64 us -> 5.07 us  [the longest x1 1.85 us: per_device(): call(input_grad_kernel, [((tokens // 2, width), bf)] * 2, work, [flat, ((...]
    ppermute x2 -> x1, starting transfers between devices: 3.83 us -> 1.92 us  [per_device(): got = lax.ppermute(other, 'c', [(0, 1), (1, 0)])]
    ppermute x3, waiting for transfers between devices: 4.44 us -> 5.94 us  [per_device(): got = lax.ppermute(away, 'my', [(i, i ^ bit) for i in range(8)])]
    convert_element_type x0 -> x1, other arithmetic: none -> 1.31 us  [per_device(): (mine.astype(f32) + got.astype(f32)).astype(bf).reshape(4, half // 4, cols)]
  transfers between devices with their start and end apart: 9 -> 8, of which waited for: 5 -> 4; matrix products, arithmetic and copies ran while one was open for 2% -> 3% of each run, Pallas kernels for 7% -> 2%
where the time goes in v2:
time: 120 us
  starting transfers between devices  68.1 us (57%)
  waiting for transfers between devices  25.2 us (21%)
  blocking collectives  10.3 us (9%)
  local copies, waits for them, and re-layouts  7.92 us (7%)
  Pallas kernels  5.07 us (4%)
  other arithmetic  2.31 us (2%)
    ppermute x2, starting transfers between devices, per_device(): got = lax.ppermute(away, ('zh', 'c'), pairs)  35 us
    ppermute x3, starting transfers between devices, per_device(): got = lax.ppermute(away, 'my', [(i, i ^ bit) for i in range(8)])  22.4 us
    ppermute x2, waiting for transfers between devices, per_device(): got = lax.ppermute(away, ('zh', 'c'), pairs)  13 us
    all_to_all x1, blocking collectives, per_device(): d = lax.all_to_all(d_mine, 'mx', 0, 0)  10.3 us
    unnamed x14, local copies, waits for them, and re-layouts  7.11 us
    all_to_all x1, waiting for transfers between devices, per_device(): parts = lax.all_to_all(send, 'mx', 0, 0)  6.28 us
    ppermute x3, waiting for transfers between devices, per_device(): got = lax.ppermute(away, 'my', [(i, i ^ bit) for i in range(8)])  5.94 us
    all_to_all x1, starting transfers between devices, per_device(): parts = lax.all_to_all(send, 'mx', 0, 0)  4.46 us
  transfers between devices with their start and end apart: 8, of which 4 were waited for; matrix products, arithmetic and copies ran while one was open for 3% of the time, Pallas kernels for 2%

profile of v2, /device:TPU:96, one launch (start us, length us, event | category | flops | bytes accessed | tf_op | source)
XLA Modules:
  0.0 119.7 jit_solution(2615320265102723889)
XLA Ops:
  0.6 2.2 %copy.6 = bf16[192,8,2,384]{3,1,2,0:T(8,128)(2,1)S(1)} copy(bf16[192,8,2,384]{3,2,1,0:T(2,128)(2,1)} %bitcast.12) | data formatting | bytes 4718592
  2.9 1.4 %shard_map.59 = (bf16[4,64,768]{2,1,0:T(8,128)(2,1)S(1)}, bf16[16,768]{1,0:T(8,128)(2,1)S(1)}) custom-call(bf16[256,1536]{1,0:T(8,128)(2,1)S(1)} %copy-done, f32[2,128]{1,0:T(2,128)S(1)} %bitcast.9, bf16[1536,768]{1,0:T(8,128)(2,1)S(1)} %bitcast.6), custom_call_target="tpu_custom_call" | custom-call | flops 603979776 | bytes 4194304 | tf_op jit(solution)/shard_map/pallas_call | solution.py:147
  4.3 0.8 copy-done.2
  5.6 4.5 %all-to-all-start = ((bf16[4,64,768]{2,1,0:T(8,128)(2,1)}), bf16[4,64,768]{2,1,0:T(8,128)(2,1)S(1)}, u32[]{:S(2)}, u32[]{:S(2)}) async-start(bf16[4,64,768]{2,1,0:T(8,128)(2,1)} %copy-done.2), calls=%async_computation | async-start | bytes 786432 | tf_op jit(solution)/shard_map/all_to_all | solution.py:148
  10.1 1.8 %copy.7 = bf16[32,8,2,384]{3,1,2,0:T(8,128)(2,1)} copy(bf16[32,8,2,384]{3,2,1,0:T(2,128)(2,1)} %bitcast.13) | data formatting | bytes 786432
  11.9 6.3 %all-to-all-done.parts_ref = bf16[4,64,768]{2,1,0:T(8,128)(2,1)S(1)} async-done(((bf16[4,64,768]{2,1,0:T(8,128)(2,1)}), bf16[4,64,768]{2,1,0:T(8,128)(2,1)S(1)}, u32[]{:S(2)}, u32[]{:S(2)}) %all-to-all-start) | async-done | bytes 393248 | tf_op jit(solution)/shard_map/all_to_all | solution.py:148
  18.2 1.0 copy-done.1
  19.2 0.7 copy-done.4
  20.4 10.3 %all_to_all.15.d_ref = bf16[4,80,768]{2,1,0:T(8,128)(2,1)S(1)} all-to-all(bf16[4,80,768]{2,1,0:T(8,128)(2,1)S(1)} %shard_map.60), channel_id=1, replica_groups=mesh['x'=4,'zh'=4,'c'=2,'mx'=4,'my'=8] {'mx'}, dimensions={0} | all-to-all | bytes 983040 | tf_op jit(solution)/shard_map/all_to_all | solution.py:150
  30.7 1.4 %shard_map.62 = (bf16[768,768]{1,0:T(8,128)(2,1)S(1)}, bf16[768,768]{1,0:T(8,128)(2,1)S(1)}) custom-call(bf16[4,80,768]{2,1,0:T(8,128)(2,1)S(1)} %all_to_all.15.d_ref, bf16[256,1536]{1,0:T(8,128)(2,1)S(1)} %copy-done, f32[2,128]{1,0:T(2,128)S(1)} %bitcast.10), custom_call_target="tpu_custom_call" | custom-call | flops 603979776 | bytes 4194304 | tf_op jit(solution)/shard_map/pallas_call | solution.py:152
  32.1 1.9 %collective-permute-start.3 = (bf16[768,768]{1,0:T(8,128)(2,1)S(1)}, bf16[768,768]{1,0:T(8,128)(2,1)S(1)}, u32[]{:S(2)}, u32[]{:S(2)}) collective-permute-start(bf16[768,768]{1,0:T(8,128)(2,1)S(1)} %get-tuple-element.13), channel_id=1, source_target_pairs={{0,32},{32,0},{1,33},{33,1},{2,34},{34,2},{3,35},{35,3},{4,36},{36... | collective-permute-start | bytes 3538952 | tf_op jit(solution)/shard_map/ppermute | solution.py:155
  34.0 1.9 %shard_map.61 = (bf16[128,1536]{1,0:T(8,128)(2,1)S(1)}, bf16[128,1536]{1,0:T(8,128)(2,1)}) custom-call(bf16[4,80,768]{2,1,0:T(8,128)(2,1)S(1)} %all_to_all.15.d_ref, bf16[1536,768]{1,0:T(8,128)(2,1)S(1)} %bitcast.7, bf16[256,1536]{1,0:T(8,128)(2,1)S(1)} %copy-done, f32[2,128]{1,0:T(2,128)S(1)} %bitcast.11), custom_call_target="tpu_custom_call" | custom-call | flops 603979776 | bytes 4194304 | tf_op jit(solution)/shard_map/pallas_call | solution.py:156
  35.9 2.0 %collective-permute-start = (bf16[128,1536]{1,0:T(8,128)(2,1)}, bf16[128,1536]{1,0:T(8,128)(2,1)S(1)}, u32[]{:S(2)}, u32[]{:S(2)}) collective-permute-start(bf16[128,1536]{1,0:T(8,128)(2,1)} %get-tuple-element.11), channel_id=1, source_target_pairs={{0,1},{1,0},{2,3},{3,2},{4,5},{5,4},{6,7},{7,6},{8,9},{9,8},{10,11... | collective-permute-start | bytes 1179656 | tf_op jit(solution)/shard_map/ppermute | solution.py:162
  37.9 1.3 %add_convert_fusion = bf16[768,768]{1,0:T(8,128)(2,1)} fusion(bf16[768,768]{1,0:T(8,128)(2,1)S(1)} %collective-permute-done.3, bf16[768,768]{1,0:T(8,128)(2,1)S(1)} %get-tuple-element.12), kind=kLoop, calls=%fused_computation.1 | loop fusion | flops 2359296 | bytes 3538944 | tf_op jit(solution)/shard_map/convert_element_type | solution.py:159
  39.2 4.3 %all-to-all-start.2 = ((bf16[4,192,768]{2,1,0:T(8,128)(2,1)}), bf16[4,192,768]{2,1,0:T(8,128)(2,1)S(1)}, u32[]{:S(2)}, u32[]{:S(2)}) async-start(bf16[4,192,768]{2,1,0:T(8,128)(2,1)} %bitcast.1), calls=%async_computation.2 | async-start | bytes 2359296 | tf_op jit(solution)/shard_map/all_to_all | solution.py:169
  43.5 5.9 %collective-permute-done = bf16[128,1536]{1,0:T(8,128)(2,1)S(1)} collective-permute-done((bf16[128,1536]{1,0:T(8,128)(2,1)}, bf16[128,1536]{1,0:T(8,128)(2,1)S(1)}, u32[]{:S(2)}, u32[]{:S(2)}) %collective-permute-start) | collective-permute-done | bytes 393248 | tf_op jit(solution)/shard_map/ppermute | solution.py:162
  49.6 11.3 %collective-permute-start.1 = (bf16[64,1536]{1,0:T(8,128)(2,1)S(1)}, bf16[64,1536]{1,0:T(8,128)(2,1)S(1)}, u32[]{:S(2)}, u32[]{:S(2)}) collective-permute-start(bf16[64,1536]{1,0:T(8,128)(2,1)S(1)} %slice.54), channel_id=1, source_target_pairs={{0,2},{1,3},{2,0},{3,1},{4,6},{5,7},{6,4},{7,5},{8,10},{9,11},{10,... | collective-permute-start | bytes 589832 | tf_op jit(solution)/shard_map/ppermute | solution.py:162
  61.1 15.4 %collective-permute-start.4 = (bf16[96,768]{1,0:T(8,128)(2,1)S(1)}, bf16[96,768]{1,0:T(8,128)(2,1)S(1)}, u32[]{:S(2)}, u32[]{:S(2)}) collective-permute-start(bf16[96,768]{1,0:T(8,128)(2,1)S(1)} %slice.55), channel_id=1, source_target_pairs={{0,64},{32,224},{64,0},{96,160},{128,192},{160,96},{192,128},{224,... | collective-permute-start | bytes 442376 | tf_op jit(solution)/shard_map/ppermute | solution.py:179
  76.6 9.1 %collective-permute-start.2 = (bf16[32,1536]{1,0:T(8,128)(2,1)S(1)}, bf16[32,1536]{1,0:T(8,128)(2,1)S(1)}, u32[]{:S(2)}, u32[]{:S(2)}) collective-permute-start(bf16[32,1536]{1,0:T(8,128)(2,1)S(1)} %slice.56), channel_id=1, source_target_pairs={{0,4},{1,5},{2,6},{3,7},{4,0},{5,1},{6,2},{7,3},{8,12},{9,13},{10,... | collective-permute-start | bytes 294920 | tf_op jit(solution)/shard_map/ppermute | solution.py:162
  85.7 10.7 %collective-permute-done.4 = bf16[96,768]{1,0:T(8,128)(2,1)S(1)} collective-permute-done((bf16[96,768]{1,0:T(8,128)(2,1)S(1)}, bf16[96,768]{1,0:T(8,128)(2,1)S(1)}, u32[]{:S(2)}, u32[]{:S(2)}) %collective-permute-start.4) | collective-permute-done | bytes 147488 | tf_op jit(solution)/shard_map/ppermute | solution.py:179
  96.4 19.6 %collective-permute-start.5 = (bf16[48,768]{1,0:T(8,128)(2,1)S(1)}, bf16[48,768]{1,0:T(8,128)(2,1)S(1)}, u32[]{:S(2)}, u32[]{:S(2)}) collective-permute-start(bf16[48,768]{1,0:T(8,128)(2,1)S(1)} %slice.57), channel_id=1, source_target_pairs={{0,192},{32,96},{64,128},{96,32},{128,64},{160,224},{192,0},{224,1... | collective-permute-start | bytes 221192 | tf_op jit(solution)/shard_map/ppermute | solution.py:179
  116.0 0.7 fusion
  116.6 2.3 %collective-permute-done.5 = bf16[48,768]{1,0:T(8,128)(2,1)S(1)} collective-permute-done((bf16[48,768]{1,0:T(8,128)(2,1)S(1)}, bf16[48,768]{1,0:T(8,128)(2,1)S(1)}, u32[]{:S(2)}, u32[]{:S(2)}) %collective-permute-start.5) | collective-permute-done | bytes 73760 | tf_op jit(solution)/shard_map/ppermute | solution.py:179
  119.0 0.7 reshape.23
  (23 shorter events, 1.5 us)
Async XLA Ops:
  0.6 2.2 %copy-start = (bf16[256,1536]{1,0:T(8,128)(2,1)S(1)}, bf16[256,1536]{1,0:T(8,128)(2,1)}, u32[]{:S(2)}) copy-start(bf16[256,1536]{1,0:T(8,128)(2,1)} %x_ref.5) | copy-start | bytes 2359300
  0.6 2.2 %copy-start.5 = (f32[256]{0:T(256)S(1)}, f32[256]{0:T(256)}, u32[]{:S(2)}) copy-start(f32[256]{0:T(256)} %param.5) | copy-start | bytes 3076
  4.2 0.8 copy-start.2
  5.0 0.6 copy-start.3
  5.6 12.5 %all-to-all-start = ((bf16[4,64,768]{2,1,0:T(8,128)(2,1)}), bf16[4,64,768]{2,1,0:T(8,128)(2,1)S(1)}, u32[]{:S(2)}, u32[]{:S(2)}) async-start(bf16[4,64,768]{2,1,0:T(8,128)(2,1)} %copy-done.2), calls=%async_computation | async-start | bytes 786432 | tf_op jit(solution)/shard_map/all_to_all | solution.py:148
  18.2 1.0 copy-start.1
  19.2 0.7 copy-start.4
  32.1 5.8 %collective-permute-start.3 = (bf16[768,768]{1,0:T(8,128)(2,1)S(1)}, bf16[768,768]{1,0:T(8,128)(2,1)S(1)}, u32[]{:S(2)}, u32[]{:S(2)}) collective-permute-start(bf16[768,768]{1,0:T(8,128)(2,1)S(1)} %get-tuple-element.13), channel_id=1, source_target_pairs={{0,32},{32,0},{1,33},{33,1},{2,34},{34,2},{3,35},{35,3},{4,36},{36... | collective-permute-start | bytes 3538952 | tf_op jit(solution)/shard_map/ppermute | solution.py:155
  35.9 13.6 %collective-permute-start = (bf16[128,1536]{1,0:T(8,128)(2,1)}, bf16[128,1536]{1,0:T(8,128)(2,1)S(1)}, u32[]{:S(2)}, u32[]{:S(2)}) collective-permute-start(bf16[128,1536]{1,0:T(8,128)(2,1)} %get-tuple-element.11), channel_id=1, source_target_pairs={{0,1},{1,0},{2,3},{3,2},{4,5},{5,4},{6,7},{7,6},{8,9},{9,8},{10,11... | collective-permute-start | bytes 1179656 | tf_op jit(solution)/shard_map/ppermute | solution.py:162
  39.2 21.7 %all-to-all-start.2 = ((bf16[4,192,768]{2,1,0:T(8,128)(2,1)}), bf16[4,192,768]{2,1,0:T(8,128)(2,1)S(1)}, u32[]{:S(2)}, u32[]{:S(2)}) async-start(bf16[4,192,768]{2,1,0:T(8,128)(2,1)} %bitcast.1), calls=%async_computation.2 | async-start | bytes 2359296 | tf_op jit(solution)/shard_map/all_to_all | solution.py:169
  49.6 26.9 %collective-permute-start.1 = (bf16[64,1536]{1,0:T(8,128)(2,1)S(1)}, bf16[64,1536]{1,0:T(8,128)(2,1)S(1)}, u32[]{:S(2)}, u32[]{:S(2)}) collective-permute-start(bf16[64,1536]{1,0:T(8,128)(2,1)S(1)} %slice.54), channel_id=1, source_target_pairs={{0,2},{1,3},{2,0},{3,1},{4,6},{5,7},{6,4},{7,5},{8,10},{9,11},{10,... | collective-permute-start | bytes 589832 | tf_op jit(solution)/shard_map/ppermute | solution.py:162
  61.1 35.3 %collective-permute-start.4 = (bf16[96,768]{1,0:T(8,128)(2,1)S(1)}, bf16[96,768]{1,0:T(8,128)(2,1)S(1)}, u32[]{:S(2)}, u32[]{:S(2)}) collective-permute-start(bf16[96,768]{1,0:T(8,128)(2,1)S(1)} %slice.55), channel_id=1, source_target_pairs={{0,64},{32,224},{64,0},{96,160},{128,192},{160,96},{192,128},{224,... | collective-permute-start | bytes 442376 | tf_op jit(solution)/shard_map/ppermute | solution.py:179
  76.6 39.4 %collective-permute-start.2 = (bf16[32,1536]{1,0:T(8,128)(2,1)S(1)}, bf16[32,1536]{1,0:T(8,128)(2,1)S(1)}, u32[]{:S(2)}, u32[]{:S(2)}) collective-permute-start(bf16[32,1536]{1,0:T(8,128)(2,1)S(1)} %slice.56), channel_id=1, source_target_pairs={{0,4},{1,5},{2,6},{3,7},{4,0},{5,1},{6,2},{7,3},{8,12},{9,13},{10,... | collective-permute-start | bytes 294920 | tf_op jit(solution)/shard_map/ppermute | solution.py:162
  96.4 22.6 %collective-permute-start.5 = (bf16[48,768]{1,0:T(8,128)(2,1)S(1)}, bf16[48,768]{1,0:T(8,128)(2,1)S(1)}, u32[]{:S(2)}, u32[]{:S(2)}) collective-permute-start(bf16[48,768]{1,0:T(8,128)(2,1)S(1)} %slice.57), channel_id=1, source_target_pairs={{0,192},{32,96},{64,128},{96,32},{128,64},{160,224},{192,0},{224,1... | collective-permute-start | bytes 221192 | tf_op jit(solution)/shard_map/ppermute | solution.py:179

commit v3 on v2

--- a/solution.py
+++ b/solution.py
@@ -117,11 +117,11 @@
     z, c = lax.axis_index("zh"), lax.axis_index("c")
     for core, out in ((1 - c, away_ref), (c, mine_ref)):
         first, second = pairings(z, core)
-        for x in range(4):
-            for place, target in enumerate((z, second, first, lax.bitwise_xor(z, 2))):
-                row0 = pl.multiple_of(((x * 4 + target) * 2 + core) * BLOCK, BLOCK)
-                at = (x * 4 + place) * BLOCK
-                out[at : at + BLOCK, :] = total[pl.ds(row0, BLOCK), :].astype(out.dtype)
+        order = [(x, lax.bitwise_xor(z, 2)) for x in range(4)]
+        order += [(x, target) for x in range(4) for target in (z, second, first)]
+        for place, (x, target) in enumerate(order):
+            row0 = pl.multiple_of(((x * 4 + target) * 2 + core) * BLOCK, BLOCK)
+            out[place * BLOCK : (place + 1) * BLOCK, :] = total[pl.ds(row0, BLOCK), :].astype(out.dtype)
 
 
 def call(kernel, outs, flops, scratch=()):
@@ -156,7 +156,8 @@
     keep, away = call(
         input_grad_kernel, [((tokens // 2, width), bf)] * 2, work, [flat, ((tokens, width), f32)]
     )(d, w, x, mean)
-    dw = (mine.astype(f32) + got.astype(f32)).astype(bf).reshape(4, half // 4, cols)
+    dw = (mine.astype(f32) + got.astype(f32)).astype(bf)
+    relay, rest = dw[: 4 * BLOCK].reshape(4, BLOCK, cols), dw[4 * BLOCK :].reshape(4, 3 * BLOCK, cols)
 
     for bit in (1, 2, 4):
         got = lax.ppermute(away, "my", [(i, i ^ bit) for i in range(8)])
@@ -166,18 +167,22 @@
             keep, away = total[:n], total[n:].astype(bf)
     input_grad = total.astype(bf)
 
-    got = lax.all_to_all(dw, "x", 0, 0)
-    total = jnp.sum(got.astype(f32), axis=0)
-    for step in range(2):
-        n = total.shape[0] // 2
-        keep, away = total[:n], total[n:].astype(bf)
+    def swap_zh(chunk, step):
         pairs = []
         for z in range(4):
             for c in range(2):
                 partner = (z ^ 1) if step == c else 3 - z
                 pairs.append((2 * z + c, 2 * partner + c))
-        got = lax.ppermute(away, ("zh", "c"), pairs)
-        total = keep + got.astype(f32)
+        return lax.ppermute(chunk, ("zh", "c"), pairs).astype(f32)
+
+    def over_x(parts):
+        return jnp.sum(lax.all_to_all(parts, "x", 0, 0).astype(f32), axis=0)
+
+    relayed = swap_zh(over_x(relay).astype(bf), 0)
+    rest = over_x(rest)
+    own, passed, straight = rest[:BLOCK], rest[BLOCK : 2 * BLOCK], rest[2 * BLOCK :]
+    own = own + swap_zh(straight.astype(bf), 0)
+    total = own + swap_zh((passed + relayed).astype(bf), 1)
     return input_grad, total.reshape(BLOCK, 2, cols // 2)
 
 

time: 120 us -> 117 us (0.975)
  the two profiles are of different devices: /device:TPU:96 before, /device:TPU:6 now
where the time goes in v3:
time: 117 us; the launch traced here: 116 us
  starting transfers between devices  69.9 us (60%)
  waiting for transfers between devices  19.5 us (17%)
  blocking collectives  10.3 us (9%)
  local copies, waits for them, and re-layouts  9.62 us (8%)
  Pallas kernels  5.07 us (4%)
  other arithmetic  1.28 us (1%)
    ppermute x3, starting transfers between devices, swap_zh(): return lax.ppermute(chunk, ('zh', 'c'), pairs).astype(f32)  31.7 us
    all_to_all x2, starting transfers between devices, over_x(): return jnp.sum(lax.all_to_all(parts, 'x', 0, 0).astype(f32), axis=0)  21.2 us
    ppermute x3, starting transfers between devices, per_device(): got = lax.ppermute(away, 'my', [(i, i ^ bit) for i in range(8)])  10.7 us
    all_to_all x1, blocking collectives, per_device(): d = lax.all_to_all(d_mine, 'mx', 0, 0)  10.3 us
    ppermute x3, waiting for transfers between devices, swap_zh(): return lax.ppermute(chunk, ('zh', 'c'), pairs).astype(f32)  9.91 us
    unnamed x14, local copies, waits for them, and re-layouts  7.11 us
    all_to_all x1, waiting for transfers between devices, per_device(): parts = lax.all_to_all(send, 'mx', 0, 0)  6.28 us
    all_to_all x1, starting transfers between devices, per_device(): parts = lax.all_to_all(send, 'mx', 0, 0)  4.46 us
  transfers between devices with their start and end apart: 10, of which 6 were waited for; matrix products, arithmetic and copies ran while one was open for 4% of the time, Pallas kernels for 2%

profile of v3, /device:TPU:6, one launch (start us, length us, event | category | flops | bytes accessed | tf_op | source)
XLA Modules:
  0.0 116.5 jit_solution(17211278565636168812)
XLA Ops:
  0.6 2.2 %copy.6 = bf16[192,8,2,384]{3,1,2,0:T(8,128)(2,1)S(1)} copy(bf16[192,8,2,384]{3,2,1,0:T(2,128)(2,1)} %bitcast.13) | data formatting | bytes 4718592
  2.9 1.4 %shard_map.59 = (bf16[4,64,768]{2,1,0:T(8,128)(2,1)S(1)}, bf16[16,768]{1,0:T(8,128)(2,1)S(1)}) custom-call(bf16[256,1536]{1,0:T(8,128)(2,1)S(1)} %copy-done, f32[2,128]{1,0:T(2,128)S(1)} %bitcast.10, bf16[1536,768]{1,0:T(8,128)(2,1)S(1)} %bitcast.7), custom_call_target="tpu_custom_call" | custom-call | flops 603979776 | bytes 4194304 | tf_op jit(solution)/shard_map/pallas_call | solution.py:147
  4.3 0.8 copy-done.2
  5.6 4.5 %all-to-all-start = ((bf16[4,64,768]{2,1,0:T(8,128)(2,1)}), bf16[4,64,768]{2,1,0:T(8,128)(2,1)S(1)}, u32[]{:S(2)}, u32[]{:S(2)}) async-start(bf16[4,64,768]{2,1,0:T(8,128)(2,1)} %copy-done.2), calls=%async_computation | async-start | bytes 786432 | tf_op jit(solution)/shard_map/all_to_all | solution.py:148
  10.1 1.8 %copy.7 = bf16[32,8,2,384]{3,1,2,0:T(8,128)(2,1)} copy(bf16[32,8,2,384]{3,2,1,0:T(2,128)(2,1)} %bitcast.14) | data formatting | bytes 786432
  11.9 6.3 %all-to-all-done.parts_ref = bf16[4,64,768]{2,1,0:T(8,128)(2,1)S(1)} async-done(((bf16[4,64,768]{2,1,0:T(8,128)(2,1)}), bf16[4,64,768]{2,1,0:T(8,128)(2,1)S(1)}, u32[]{:S(2)}, u32[]{:S(2)}) %all-to-all-start) | async-done | bytes 393248 | tf_op jit(solution)/shard_map/all_to_all | solution.py:148
  18.2 1.0 copy-done.1
  20.4 10.3 %all_to_all.20.d_ref = bf16[4,80,768]{2,1,0:T(8,128)(2,1)S(1)} all-to-all(bf16[4,80,768]{2,1,0:T(8,128)(2,1)S(1)} %shard_map.60), channel_id=1, replica_groups=mesh['x'=4,'zh'=4,'c'=2,'mx'=4,'my'=8] {'mx'}, dimensions={0} | all-to-all | bytes 983040 | tf_op jit(solution)/shard_map/all_to_all | solution.py:150
  30.7 1.4 %shard_map.62 = (bf16[768,768]{1,0:T(8,128)(2,1)S(1)}, bf16[768,768]{1,0:T(8,128)(2,1)S(1)}) custom-call(bf16[4,80,768]{2,1,0:T(8,128)(2,1)S(1)} %all_to_all.20.d_ref, bf16[256,1536]{1,0:T(8,128)(2,1)S(1)} %copy-done, f32[2,128]{1,0:T(2,128)S(1)} %bitcast.11), custom_call_target="tpu_custom_call" | custom-call | flops 603979776 | bytes 4194304 | tf_op jit(solution)/shard_map/pallas_call | solution.py:152
  32.1 1.9 %collective-permute-start.3 = (bf16[768,768]{1,0:T(8,128)(2,1)S(1)}, bf16[768,768]{1,0:T(8,128)(2,1)S(1)}, u32[]{:S(2)}, u32[]{:S(2)}) collective-permute-start(bf16[768,768]{1,0:T(8,128)(2,1)S(1)} %get-tuple-element.13), channel_id=1, source_target_pairs={{0,32},{32,0},{1,33},{33,1},{2,34},{34,2},{3,35},{35,3},{4,36},{36... | collective-permute-start | bytes 3538952 | tf_op jit(solution)/shard_map/ppermute | solution.py:155
  34.0 1.9 %shard_map.61 = (bf16[128,1536]{1,0:T(8,128)(2,1)S(1)}, bf16[128,1536]{1,0:T(8,128)(2,1)}) custom-call(bf16[4,80,768]{2,1,0:T(8,128)(2,1)S(1)} %all_to_all.20.d_ref, bf16[1536,768]{1,0:T(8,128)(2,1)S(1)} %bitcast.8, bf16[256,1536]{1,0:T(8,128)(2,1)S(1)} %copy-done, f32[2,128]{1,0:T(2,128)S(1)} %bitcast.12), custom_call_target="tpu_custom_call" | custom-call | flops 603979776 | bytes 4194304 | tf_op jit(solution)/shard_map/pallas_call | solution.py:156
  35.8 3.8 %collective-permute-start = (bf16[128,1536]{1,0:T(8,128)(2,1)}, bf16[128,1536]{1,0:T(8,128)(2,1)S(1)}, u32[]{:S(2)}, u32[]{:S(2)}) collective-permute-start(bf16[128,1536]{1,0:T(8,128)(2,1)} %get-tuple-element.11), channel_id=1, source_target_pairs={{0,1},{1,0},{2,3},{3,2},{4,5},{5,4},{6,7},{7,6},{8,9},{9,8},{10,11... | collective-permute-start | bytes 1179656 | tf_op jit(solution)/shard_map/ppermute | solution.py:163
  40.0 0.7 slice.47
  40.7 13.3 %all-to-all-start.3 = ((bf16[4,48,768]{2,1,0:T(8,128)(2,1)}), bf16[4,48,768]{2,1,0:T(8,128)(2,1)S(1)}, u32[]{:S(2)}, u32[]{:S(2)}) async-start(bf16[4,48,768]{2,1,0:T(8,128)(2,1)} %bitcast.2), calls=%async_computation.3 | async-start | bytes 589824 | tf_op jit(solution)/shard_map/all_to_all | solution.py:179
  54.2 1.9 %collective-permute-start.1 = (bf16[64,1536]{1,0:T(8,128)(2,1)S(1)}, bf16[64,1536]{1,0:T(8,128)(2,1)S(1)}, u32[]{:S(2)}, u32[]{:S(2)}) collective-permute-start(bf16[64,1536]{1,0:T(8,128)(2,1)S(1)} %slice.61), channel_id=1, source_target_pairs={{0,2},{1,3},{2,0},{3,1},{4,6},{5,7},{6,4},{7,5},{8,10},{9,11},{10,... | collective-permute-start | bytes 589832 | tf_op jit(solution)/shard_map/ppermute | solution.py:163
  56.1 1.0 slice.43
  57.1 2.8 %all-to-all-done.3 = bf16[4,48,768]{2,1,0:T(8,128)(2,1)S(1)} async-done(((bf16[4,48,768]{2,1,0:T(8,128)(2,1)}), bf16[4,48,768]{2,1,0:T(8,128)(2,1)S(1)}, u32[]{:S(2)}, u32[]{:S(2)}) %all-to-all-start.3) | async-done | bytes 294944 | tf_op jit(solution)/shard_map/all_to_all | solution.py:179
  59.9 7.8 %all-to-all-start.2 = ((bf16[4,144,768]{2,1,0:T(8,128)(2,1)}), bf16[4,144,768]{2,1,0:T(8,128)(2,1)S(1)}, u32[]{:S(2)}, u32[]{:S(2)}) async-start(bf16[4,144,768]{2,1,0:T(8,128)(2,1)} %bitcast.1), calls=%async_computation.2 | async-start | bytes 1769472 | tf_op jit(solution)/shard_map/all_to_all | solution.py:179
  68.3 4.9 %collective-permute-start.2 = (bf16[32,1536]{1,0:T(8,128)(2,1)S(1)}, bf16[32,1536]{1,0:T(8,128)(2,1)S(1)}, u32[]{:S(2)}, u32[]{:S(2)}) collective-permute-start(bf16[32,1536]{1,0:T(8,128)(2,1)S(1)} %slice.62), channel_id=1, source_target_pairs={{0,4},{1,5},{2,6},{3,7},{4,0},{5,1},{6,2},{7,3},{8,12},{9,13},{10,... | collective-permute-start | bytes 294920 | tf_op jit(solution)/shard_map/ppermute | solution.py:163
  73.3 15.7 %collective-permute-start.5 = (bf16[48,768]{1,0:T(8,128)(2,1)S(1)}, bf16[48,768]{1,0:T(8,128)(2,1)S(1)}, u32[]{:S(2)}, u32[]{:S(2)}) collective-permute-start(bf16[48,768]{1,0:T(8,128)(2,1)S(1)} %reduce_sum.22), channel_id=1, source_target_pairs={{0,64},{32,224},{64,0},{96,160},{128,192},{160,96},{192,128},{224,... | collective-permute-start | bytes 221192 | tf_op jit(solution)/shard_map/ppermute | solution.py:176
  89.2 1.9 %collective-permute-start.4 = (bf16[48,768]{1,0:T(8,128)(2,1)S(1)}, bf16[48,768]{1,0:T(8,128)(2,1)S(1)}, u32[]{:S(2)}, u32[]{:S(2)}) collective-permute-start(bf16[48,768]{1,0:T(8,128)(2,1)S(1)} %slice.63), channel_id=1, source_target_pairs={{0,64},{32,224},{64,0},{96,160},{128,192},{160,96},{192,128},{224,... | collective-permute-start | bytes 221192 | tf_op jit(solution)/shard_map/ppermute | solution.py:176
  91.1 4.1 %collective-permute-done.5 = bf16[48,768]{1,0:T(8,128)(2,1)S(1)} collective-permute-done((bf16[48,768]{1,0:T(8,128)(2,1)S(1)}, bf16[48,768]{1,0:T(8,128)(2,1)S(1)}, u32[]{:S(2)}, u32[]{:S(2)}) %collective-permute-start.5) | collective-permute-done | bytes 73760 | tf_op jit(solution)/shard_map/ppermute | solution.py:176
  95.2 14.0 %collective-permute-start.6 = (bf16[48,768]{1,0:T(8,128)(2,1)S(1)}, bf16[48,768]{1,0:T(8,128)(2,1)S(1)}, u32[]{:S(2)}, u32[]{:S(2)}) collective-permute-start(bf16[48,768]{1,0:T(8,128)(2,1)S(1)} %fusion.1), channel_id=1, source_target_pairs={{0,192},{32,96},{64,128},{96,32},{128,64},{160,224},{192,0},{224,1... | collective-permute-start | bytes 221192 | tf_op jit(solution)/shard_map/ppermute | solution.py:176
  110.4 5.3 %collective-permute-done.6 = bf16[48,768]{1,0:T(8,128)(2,1)S(1)} collective-permute-done((bf16[48,768]{1,0:T(8,128)(2,1)S(1)}, bf16[48,768]{1,0:T(8,128)(2,1)S(1)}, u32[]{:S(2)}, u32[]{:S(2)}) %collective-permute-start.6) | collective-permute-done | bytes 73760 | tf_op jit(solution)/shard_map/ppermute | solution.py:176
  (29 shorter events, 4.8 us)
Async XLA Ops:
  0.6 2.2 %copy-start = (bf16[256,1536]{1,0:T(8,128)(2,1)S(1)}, bf16[256,1536]{1,0:T(8,128)(2,1)}, u32[]{:S(2)}) copy-start(bf16[256,1536]{1,0:T(8,128)(2,1)} %x_ref.5) | copy-start | bytes 2359300
  0.6 2.2 %copy-start.5 = (f32[256]{0:T(256)S(1)}, f32[256]{0:T(256)}, u32[]{:S(2)}) copy-start(f32[256]{0:T(256)} %param.5) | copy-start | bytes 3076
  4.2 0.8 copy-start.2
  5.0 0.6 copy-start.3
  5.6 12.5 %all-to-all-start = ((bf16[4,64,768]{2,1,0:T(8,128)(2,1)}), bf16[4,64,768]{2,1,0:T(8,128)(2,1)S(1)}, u32[]{:S(2)}, u32[]{:S(2)}) async-start(bf16[4,64,768]{2,1,0:T(8,128)(2,1)} %copy-done.2), calls=%async_computation | async-start | bytes 786432 | tf_op jit(solution)/shard_map/all_to_all | solution.py:148
  18.2 1.0 copy-start.1
  19.2 0.7 copy-start.4
  32.1 7.6 %collective-permute-start.3 = (bf16[768,768]{1,0:T(8,128)(2,1)S(1)}, bf16[768,768]{1,0:T(8,128)(2,1)S(1)}, u32[]{:S(2)}, u32[]{:S(2)}) collective-permute-start(bf16[768,768]{1,0:T(8,128)(2,1)S(1)} %get-tuple-element.13), channel_id=1, source_target_pairs={{0,32},{32,0},{1,33},{33,1},{2,34},{34,2},{3,35},{35,3},{4,36},{36... | collective-permute-start | bytes 3538952 | tf_op jit(solution)/shard_map/ppermute | solution.py:155
  35.8 18.2 %collective-permute-start = (bf16[128,1536]{1,0:T(8,128)(2,1)}, bf16[128,1536]{1,0:T(8,128)(2,1)S(1)}, u32[]{:S(2)}, u32[]{:S(2)}) collective-permute-start(bf16[128,1536]{1,0:T(8,128)(2,1)} %get-tuple-element.11), channel_id=1, source_target_pairs={{0,1},{1,0},{2,3},{3,2},{4,5},{5,4},{6,7},{7,6},{8,9},{9,8},{10,11... | collective-permute-start | bytes 1179656 | tf_op jit(solution)/shard_map/ppermute | solution.py:163
  40.7 19.2 %all-to-all-start.3 = ((bf16[4,48,768]{2,1,0:T(8,128)(2,1)}), bf16[4,48,768]{2,1,0:T(8,128)(2,1)S(1)}, u32[]{:S(2)}, u32[]{:S(2)}) async-start(bf16[4,48,768]{2,1,0:T(8,128)(2,1)} %bitcast.2), calls=%async_computation.3 | async-start | bytes 589824 | tf_op jit(solution)/shard_map/all_to_all | solution.py:179
  54.2 14.0 %collective-permute-start.1 = (bf16[64,1536]{1,0:T(8,128)(2,1)S(1)}, bf16[64,1536]{1,0:T(8,128)(2,1)S(1)}, u32[]{:S(2)}, u32[]{:S(2)}) collective-permute-start(bf16[64,1536]{1,0:T(8,128)(2,1)S(1)} %slice.61), channel_id=1, source_target_pairs={{0,2},{1,3},{2,0},{3,1},{4,6},{5,7},{6,4},{7,5},{8,10},{9,11},{10,... | collective-permute-start | bytes 589832 | tf_op jit(solution)/shard_map/ppermute | solution.py:163
  59.9 29.1 %all-to-all-start.2 = ((bf16[4,144,768]{2,1,0:T(8,128)(2,1)}), bf16[4,144,768]{2,1,0:T(8,128)(2,1)S(1)}, u32[]{:S(2)}, u32[]{:S(2)}) async-start(bf16[4,144,768]{2,1,0:T(8,128)(2,1)} %bitcast.1), calls=%async_computation.2 | async-start | bytes 1769472 | tf_op jit(solution)/shard_map/all_to_all | solution.py:179
  68.3 41.0 %collective-permute-start.2 = (bf16[32,1536]{1,0:T(8,128)(2,1)S(1)}, bf16[32,1536]{1,0:T(8,128)(2,1)S(1)}, u32[]{:S(2)}, u32[]{:S(2)}) collective-permute-start(bf16[32,1536]{1,0:T(8,128)(2,1)S(1)} %slice.62), channel_id=1, source_target_pairs={{0,4},{1,5},{2,6},{3,7},{4,0},{5,1},{6,2},{7,3},{8,12},{9,13},{10,... | collective-permute-start | bytes 294920 | tf_op jit(solution)/shard_map/ppermute | solution.py:163
  73.3 22.0 %collective-permute-start.5 = (bf16[48,768]{1,0:T(8,128)(2,1)S(1)}, bf16[48,768]{1,0:T(8,128)(2,1)S(1)}, u32[]{:S(2)}, u32[]{:S(2)}) collective-permute-start(bf16[48,768]{1,0:T(8,128)(2,1)S(1)} %reduce_sum.22), channel_id=1, source_target_pairs={{0,64},{32,224},{64,0},{96,160},{128,192},{160,96},{192,128},{224,... | collective-permute-start | bytes 221192 | tf_op jit(solution)/shard_map/ppermute | solution.py:176
  89.2 21.2 %collective-permute-start.4 = (bf16[48,768]{1,0:T(8,128)(2,1)S(1)}, bf16[48,768]{1,0:T(8,128)(2,1)S(1)}, u32[]{:S(2)}, u32[]{:S(2)}) collective-permute-start(bf16[48,768]{1,0:T(8,128)(2,1)S(1)} %slice.63), channel_id=1, source_target_pairs={{0,64},{32,224},{64,0},{96,160},{128,192},{160,96},{192,128},{224,... | collective-permute-start | bytes 221192 | tf_op jit(solution)/shard_map/ppermute | solution.py:176
  95.2 20.5 %collective-permute-start.6 = (bf16[48,768]{1,0:T(8,128)(2,1)S(1)}, bf16[48,768]{1,0:T(8,128)(2,1)S(1)}, u32[]{:S(2)}, u32[]{:S(2)}) collective-permute-start(bf16[48,768]{1,0:T(8,128)(2,1)S(1)} %fusion.1), channel_id=1, source_target_pairs={{0,192},{32,96},{64,128},{96,32},{128,64},{160,224},{192,0},{224,1... | collective-permute-start | bytes 221192 | tf_op jit(solution)/shard_map/ppermute | solution.py:176

commit v4 on v2

--- a/solution.py
+++ b/solution.py
@@ -158,26 +158,30 @@
     )(d, w, x, mean)
     dw = (mine.astype(f32) + got.astype(f32)).astype(bf).reshape(4, half // 4, cols)
 
-    for bit in (1, 2, 4):
-        got = lax.ppermute(away, "my", [(i, i ^ bit) for i in range(8)])
-        total = keep.astype(f32) + got.astype(f32)
-        n = total.shape[0] // 2
-        if bit < 4:
-            keep, away = total[:n], total[n:].astype(bf)
-    input_grad = total.astype(bf)
-
-    got = lax.all_to_all(dw, "x", 0, 0)
-    total = jnp.sum(got.astype(f32), axis=0)
-    for step in range(2):
-        n = total.shape[0] // 2
-        keep, away = total[:n], total[n:].astype(bf)
+    def swap_zh(chunk, step):
         pairs = []
         for z in range(4):
             for c in range(2):
                 partner = (z ^ 1) if step == c else 3 - z
                 pairs.append((2 * z + c, 2 * partner + c))
-        got = lax.ppermute(away, ("zh", "c"), pairs)
-        total = keep + got.astype(f32)
+        return lax.ppermute(chunk.astype(bf), ("zh", "c"), pairs).astype(f32)
+
+    def swap_my(away, bit):
+        return lax.ppermute(away, "my", [(i, i ^ bit) for i in range(8)])
+
+    got = swap_my(away, 1)
+    total = jnp.sum(lax.all_to_all(dw, "x", 0, 0).astype(f32), axis=0)
+    got, total = lax.optimization_barrier((got, total))
+    own, passed, straight, relay = [total[i * BLOCK : (i + 1) * BLOCK] for i in range(4)]
+    relayed = swap_zh(relay, 0)
+    total = keep.astype(f32) + got.astype(f32)
+    n = total.shape[0] // 2
+    total = total[:n] + swap_my(total[n:].astype(bf), 2).astype(f32)
+    n //= 2
+    keep, away = total[:n], total[n:].astype(bf)
+    input_grad = (keep + swap_my(away, 4).astype(f32)).astype(bf)
+    own = own + swap_zh(straight, 0)
+    total = own + swap_zh(passed + relayed, 1)
     return input_grad, total.reshape(BLOCK, 2, cols // 2)
 
 

time: 120 us -> 122 us (1.017)
  the two profiles are of different devices: /device:TPU:96 before, /device:TPU:1 now
where the time goes in v4:
time: 122 us; the launch traced here: 121 us
  starting transfers between devices  59.3 us (49%)
  waiting for transfers between devices  33.9 us (28%)
  blocking collectives  9.49 us (8%)
  local copies, waits for them, and re-layouts  8.91 us (7%)
  Pallas kernels  5.08 us (4%)
  other arithmetic  3.64 us (3%)
    ppermute x3, starting transfers between devices, swap_zh(): return lax.ppermute(chunk.astype(bf), ('zh', 'c'), pairs).astype(f32)  25.8 us
    ppermute x1, starting transfers between devices, per_device(): got = lax.ppermute(other, 'c', [(0, 1), (1, 0)])  16.8 us
    ppermute x3, waiting for transfers between devices, swap_my(): return lax.ppermute(away, 'my', [(i, i ^ bit) for i in range(8)])  15.3 us
    all_to_all x1, waiting for transfers between devices, per_device(): total = jnp.sum(lax.all_to_all(dw, 'x', 0, 0).astype(f32), axis=0)  11.5 us
    all_to_all x1, blocking collectives, per_device(): d = lax.all_to_all(d_mine, 'mx', 0, 0)  9.49 us
    unnamed x18, local copies, waits for them, and re-layouts  8.13 us
    ppermute x3, starting transfers between devices, swap_my(): return lax.ppermute(away, 'my', [(i, i ^ bit) for i in range(8)])  7.39 us
    all_to_all x1, starting transfers between devices, per_device(): parts = lax.all_to_all(send, 'mx', 0, 0)  5.01 us
  transfers between devices with their start and end apart: 9, of which 6 were waited for; matrix products, arithmetic and copies ran while one was open for 3% of the time, Pallas kernels for 2%

profile of v4, /device:TPU:1, one launch (start us, length us, event | category | flops | bytes accessed | tf_op | source)
XLA Modules:
  0.0 121.2 jit_solution(18325717761477103595)
XLA Ops:
  0.6 2.2 %copy.6 = bf16[192,8,2,384]{3,1,2,0:T(8,128)(2,1)S(1)} copy(bf16[192,8,2,384]{3,2,1,0:T(2,128)(2,1)} %bitcast.13) | data formatting | bytes 4718592
  2.9 1.4 %shard_map.59 = (bf16[4,64,768]{2,1,0:T(8,128)(2,1)S(1)}, bf16[16,768]{1,0:T(8,128)(2,1)S(1)}) custom-call(bf16[256,1536]{1,0:T(8,128)(2,1)S(1)} %copy-done, f32[2,128]{1,0:T(2,128)S(1)} %bitcast.9, bf16[1536,768]{1,0:T(8,128)(2,1)S(1)} %bitcast.6), custom_call_target="tpu_custom_call" | custom-call | flops 603979776 | bytes 4194304 | tf_op jit(solution)/shard_map/pallas_call | solution.py:147
  5.6 5.0 %all-to-all-start = ((bf16[4,64,768]{2,1,0:T(8,128)(2,1)}), bf16[4,64,768]{2,1,0:T(8,128)(2,1)S(1)}, u32[]{:S(2)}, u32[]{:S(2)}) async-start(bf16[4,64,768]{2,1,0:T(8,128)(2,1)} %copy-done.4), calls=%async_computation | async-start | bytes 786432 | tf_op jit(solution)/shard_map/all_to_all | solution.py:148
  10.6 1.8 %copy.7 = bf16[32,8,2,384]{3,1,2,0:T(8,128)(2,1)} copy(bf16[32,8,2,384]{3,2,1,0:T(2,128)(2,1)} %bitcast.14) | data formatting | bytes 786432
  12.4 4.4 %all-to-all-done.parts_ref = bf16[4,64,768]{2,1,0:T(8,128)(2,1)S(1)} async-done(((bf16[4,64,768]{2,1,0:T(8,128)(2,1)}), bf16[4,64,768]{2,1,0:T(8,128)(2,1)S(1)}, u32[]{:S(2)}, u32[]{:S(2)}) %all-to-all-start) | async-done | bytes 393248 | tf_op jit(solution)/shard_map/all_to_all | solution.py:148
  16.9 1.0 copy-done.3
  19.1 9.5 %all_to_all.15.d_ref = bf16[4,80,768]{2,1,0:T(8,128)(2,1)S(1)} all-to-all(bf16[4,80,768]{2,1,0:T(8,128)(2,1)S(1)} %shard_map.60), channel_id=1, replica_groups=mesh['x'=4,'zh'=4,'c'=2,'mx'=4,'my'=8] {'mx'}, dimensions={0} | all-to-all | bytes 983040 | tf_op jit(solution)/shard_map/all_to_all | solution.py:150
  28.5 1.4 %shard_map.62 = (bf16[768,768]{1,0:T(8,128)(2,1)S(1)}, bf16[768,768]{1,0:T(8,128)(2,1)S(1)}) custom-call(bf16[4,80,768]{2,1,0:T(8,128)(2,1)S(1)} %all_to_all.15.d_ref, bf16[256,1536]{1,0:T(8,128)(2,1)S(1)} %copy-done, f32[2,128]{1,0:T(2,128)S(1)} %bitcast.10), custom_call_target="tpu_custom_call" | custom-call | flops 603979776 | bytes 4194304 | tf_op jit(solution)/shard_map/pallas_call | solution.py:152
  29.9 16.8 %collective-permute-start.1 = (bf16[768,768]{1,0:T(8,128)(2,1)S(1)}, bf16[768,768]{1,0:T(8,128)(2,1)S(1)}, u32[]{:S(2)}, u32[]{:S(2)}) collective-permute-start(bf16[768,768]{1,0:T(8,128)(2,1)S(1)} %get-tuple-element.15), channel_id=1, source_target_pairs={{0,32},{32,0},{1,33},{33,1},{2,34},{34,2},{3,35},{35,3},{4,36},{36... | collective-permute-start | bytes 3538952 | tf_op jit(solution)/shard_map/ppermute | solution.py:155
  46.8 2.5 %collective-permute-done.1 = bf16[768,768]{1,0:T(8,128)(2,1)S(1)} collective-permute-done((bf16[768,768]{1,0:T(8,128)(2,1)S(1)}, bf16[768,768]{1,0:T(8,128)(2,1)S(1)}, u32[]{:S(2)}, u32[]{:S(2)}) %collective-permute-start.1) | collective-permute-done | bytes 1179680 | tf_op jit(solution)/shard_map/ppermute | solution.py:155
  49.3 1.3 %add_convert_fusion = bf16[768,768]{1,0:T(8,128)(2,1)} fusion(bf16[768,768]{1,0:T(8,128)(2,1)S(1)} %collective-permute-done.1, bf16[768,768]{1,0:T(8,128)(2,1)S(1)} %get-tuple-element.14), kind=kLoop, calls=%fused_computation.1 | loop fusion | flops 2359296 | bytes 3538944 | tf_op jit(solution)/shard_map/convert_element_type | solution.py:159
  50.5 4.3 %all-to-all-start.2 = ((bf16[4,192,768]{2,1,0:T(8,128)(2,1)}), bf16[4,192,768]{2,1,0:T(8,128)(2,1)}, u32[]{:S(2)}, u32[]{:S(2)}) async-start(bf16[4,192,768]{2,1,0:T(8,128)(2,1)} %bitcast.12), calls=%async_computation.2 | async-start | bytes 2359296 | tf_op jit(solution)/shard_map/all_to_all | solution.py:173
  54.8 1.0 copy-done.2
  55.8 1.9 %shard_map.61 = (bf16[128,1536]{1,0:T(8,128)(2,1)S(1)}, bf16[128,1536]{1,0:T(8,128)(2,1)}) custom-call(bf16[4,80,768]{2,1,0:T(8,128)(2,1)S(1)} %copy-done.2, bf16[1536,768]{1,0:T(8,128)(2,1)S(1)} %bitcast.7, bf16[256,1536]{1,0:T(8,128)(2,1)S(1)} %copy-done, f32[2,128]{1,0:T(2,128)S(1)} %bitcast.11), custom_call_target="tpu_custom_call" | custom-call | flops 603979776 | bytes 4194304 | tf_op jit(solution)/shard_map/pallas_call | solution.py:156
  57.7 1.9 %collective-permute-start = (bf16[128,1536]{1,0:T(8,128)(2,1)}, bf16[128,1536]{1,0:T(8,128)(2,1)S(1)}, u32[]{:S(2)}, u32[]{:S(2)}) collective-permute-start(bf16[128,1536]{1,0:T(8,128)(2,1)} %get-tuple-element.13), channel_id=1, source_target_pairs={{0,1},{1,0},{2,3},{3,2},{4,5},{5,4},{6,7},{7,6},{8,9},{9,8},{10,11... | collective-permute-start | bytes 1179656 | tf_op jit(solution)/shard_map/ppermute | solution.py:170
  59.6 11.5 %all-to-all-done.2 = bf16[4,192,768]{2,1,0:T(8,128)(2,1)} async-done(((bf16[4,192,768]{2,1,0:T(8,128)(2,1)}), bf16[4,192,768]{2,1,0:T(8,128)(2,1)}, u32[]{:S(2)}, u32[]{:S(2)}) %all-to-all-start.2) | async-done | bytes 1179680 | tf_op jit(solution)/shard_map/all_to_all | solution.py:173
  71.1 1.5 %convert_reduce_fusion = f32[192,768]{1,0:T(8,128)S(1)} fusion(bf16[4,192,768]{2,1,0:T(8,128)(2,1)} %all-to-all-done.2), kind=kLoop, calls=%fused_computation | loop fusion | flops 1032192 | bytes 1769472 | tf_op jit(solution)/shard_map/reduce_sum | solution.py:173
  72.7 11.3 %collective-permute-start.5 = (bf16[48,768]{1,0:T(8,128)(2,1)S(1)}, bf16[48,768]{1,0:T(8,128)(2,1)S(1)}, u32[]{:S(2)}, u32[]{:S(2)}) collective-permute-start(bf16[48,768]{1,0:T(8,128)(2,1)S(1)} %get-tuple-element.19), channel_id=1, source_target_pairs={{0,64},{32,224},{64,0},{96,160},{128,192},{160,96},{192,128},{224,... | collective-permute-start | bytes 221192 | tf_op jit(solution)/shard_map/ppermute | solution.py:167
  84.2 3.1 %collective-permute-start.2 = (bf16[64,1536]{1,0:T(8,128)(2,1)S(1)}, bf16[64,1536]{1,0:T(8,128)(2,1)S(1)}, u32[]{:S(2)}, u32[]{:S(2)}) collective-permute-start(bf16[64,1536]{1,0:T(8,128)(2,1)S(1)} %slice.50), channel_id=1, source_target_pairs={{0,2},{1,3},{2,0},{3,1},{4,6},{5,7},{6,4},{7,5},{8,10},{9,11},{10,... | collective-permute-start | bytes 589832 | tf_op jit(solution)/shard_map/ppermute | solution.py:170
  87.2 1.9 %collective-permute-start.4 = (bf16[48,768]{1,0:T(8,128)(2,1)S(1)}, bf16[48,768]{1,0:T(8,128)(2,1)S(1)}, u32[]{:S(2)}, u32[]{:S(2)}) collective-permute-start(bf16[48,768]{1,0:T(8,128)(2,1)S(1)} %get-tuple-element.18), channel_id=1, source_target_pairs={{0,64},{32,224},{64,0},{96,160},{128,192},{160,96},{192,128},{224,... | collective-permute-start | bytes 221192 | tf_op jit(solution)/shard_map/ppermute | solution.py:167
  89.2 12.5 %collective-permute-start.6 = (bf16[48,768]{1,0:T(8,128)(2,1)S(1)}, bf16[48,768]{1,0:T(8,128)(2,1)S(1)}, u32[]{:S(2)}, u32[]{:S(2)}) collective-permute-start(bf16[48,768]{1,0:T(8,128)(2,1)S(1)} %add_convert_fusion.1), channel_id=1, source_target_pairs={{0,192},{32,96},{64,128},{96,32},{128,64},{160,224},{192,0},{224,1... | collective-permute-start | bytes 221192 | tf_op jit(solution)/shard_map/ppermute | solution.py:167
  101.7 3.2 %collective-permute-done.2 = bf16[64,1536]{1,0:T(8,128)(2,1)S(1)} collective-permute-done((bf16[64,1536]{1,0:T(8,128)(2,1)S(1)}, bf16[64,1536]{1,0:T(8,128)(2,1)S(1)}, u32[]{:S(2)}, u32[]{:S(2)}) %collective-permute-start.2) | collective-permute-done | bytes 196640 | tf_op jit(solution)/shard_map/ppermute | solution.py:170
  105.0 2.4 %collective-permute-start.3 = (bf16[32,1536]{1,0:T(8,128)(2,1)S(1)}, bf16[32,1536]{1,0:T(8,128)(2,1)S(1)}, u32[]{:S(2)}, u32[]{:S(2)}) collective-permute-start(bf16[32,1536]{1,0:T(8,128)(2,1)S(1)} %slice.51), channel_id=1, source_target_pairs={{0,4},{1,5},{2,6},{3,7},{4,0},{5,1},{6,2},{7,3},{8,12},{9,13},{10,... | collective-permute-start | bytes 294920 | tf_op jit(solution)/shard_map/ppermute | solution.py:170
  108.4 12.1 %collective-permute-done.3 = bf16[32,1536]{1,0:T(8,128)(2,1)S(1)} collective-permute-done((bf16[32,1536]{1,0:T(8,128)(2,1)S(1)}, bf16[32,1536]{1,0:T(8,128)(2,1)S(1)}, u32[]{:S(2)}, u32[]{:S(2)}) %collective-permute-start.3) | collective-permute-done | bytes 98336 | tf_op jit(solution)/shard_map/ppermute | solution.py:170
  (29 shorter events, 4.4 us)
Async XLA Ops:
  0.6 2.2 %copy-start = (bf16[256,1536]{1,0:T(8,128)(2,1)S(1)}, bf16[256,1536]{1,0:T(8,128)(2,1)}, u32[]{:S(2)}) copy-start(bf16[256,1536]{1,0:T(8,128)(2,1)} %x_ref.5) | copy-start | bytes 2359300
  0.6 2.2 %copy-start.7 = (f32[256]{0:T(256)S(1)}, f32[256]{0:T(256)}, u32[]{:S(2)}) copy-start(f32[256]{0:T(256)} %param.5) | copy-start | bytes 3076
  4.2 0.8 copy-start.4
  5.0 0.6 copy-start.5
  5.6 11.2 %all-to-all-start = ((bf16[4,64,768]{2,1,0:T(8,128)(2,1)}), bf16[4,64,768]{2,1,0:T(8,128)(2,1)S(1)}, u32[]{:S(2)}, u32[]{:S(2)}) async-start(bf16[4,64,768]{2,1,0:T(8,128)(2,1)} %copy-done.4), calls=%async_computation | async-start | bytes 786432 | tf_op jit(solution)/shard_map/all_to_all | solution.py:148
  16.9 1.0 copy-start.3
  17.9 0.7 copy-start.6
  28.5 22.0 %copy-start.1 = (bf16[4,80,768]{2,1,0:T(8,128)(2,1)}, bf16[4,80,768]{2,1,0:T(8,128)(2,1)S(1)}, u32[]{:S(2)}) copy-start(bf16[4,80,768]{2,1,0:T(8,128)(2,1)S(1)} %all_to_all.15.d_ref) | copy-start | bytes 1474564
  29.9 19.3 %collective-permute-start.1 = (bf16[768,768]{1,0:T(8,128)(2,1)S(1)}, bf16[768,768]{1,0:T(8,128)(2,1)S(1)}, u32[]{:S(2)}, u32[]{:S(2)}) collective-permute-start(bf16[768,768]{1,0:T(8,128)(2,1)S(1)} %get-tuple-element.15), channel_id=1, source_target_pairs={{0,32},{32,0},{1,33},{33,1},{2,34},{34,2},{3,35},{35,3},{4,36},{36... | collective-permute-start | bytes 3538952 | tf_op jit(solution)/shard_map/ppermute | solution.py:155
  50.5 20.6 %all-to-all-start.2 = ((bf16[4,192,768]{2,1,0:T(8,128)(2,1)}), bf16[4,192,768]{2,1,0:T(8,128)(2,1)}, u32[]{:S(2)}, u32[]{:S(2)}) async-start(bf16[4,192,768]{2,1,0:T(8,128)(2,1)} %bitcast.12), calls=%async_computation.2 | async-start | bytes 2359296 | tf_op jit(solution)/shard_map/all_to_all | solution.py:173
  54.8 1.0 copy-start.2
  57.7 14.9 %collective-permute-start = (bf16[128,1536]{1,0:T(8,128)(2,1)}, bf16[128,1536]{1,0:T(8,128)(2,1)S(1)}, u32[]{:S(2)}, u32[]{:S(2)}) collective-permute-start(bf16[128,1536]{1,0:T(8,128)(2,1)} %get-tuple-element.13), channel_id=1, source_target_pairs={{0,1},{1,0},{2,3},{3,2},{4,5},{5,4},{6,7},{7,6},{8,9},{9,8},{10,11... | collective-permute-start | bytes 1179656 | tf_op jit(solution)/shard_map/ppermute | solution.py:170
  72.7 16.5 %collective-permute-start.5 = (bf16[48,768]{1,0:T(8,128)(2,1)S(1)}, bf16[48,768]{1,0:T(8,128)(2,1)S(1)}, u32[]{:S(2)}, u32[]{:S(2)}) collective-permute-start(bf16[48,768]{1,0:T(8,128)(2,1)S(1)} %get-tuple-element.19), channel_id=1, source_target_pairs={{0,64},{32,224},{64,0},{96,160},{128,192},{160,96},{192,128},{224,... | collective-permute-start | bytes 221192 | tf_op jit(solution)/shard_map/ppermute | solution.py:167
  84.2 20.7 %collective-permute-start.2 = (bf16[64,1536]{1,0:T(8,128)(2,1)S(1)}, bf16[64,1536]{1,0:T(8,128)(2,1)S(1)}, u32[]{:S(2)}, u32[]{:S(2)}) collective-permute-start(bf16[64,1536]{1,0:T(8,128)(2,1)S(1)} %slice.50), channel_id=1, source_target_pairs={{0,2},{1,3},{2,0},{3,1},{4,6},{5,7},{6,4},{7,5},{8,10},{9,11},{10,... | collective-permute-start | bytes 589832 | tf_op jit(solution)/shard_map/ppermute | solution.py:170
  87.2 20.2 %collective-permute-start.4 = (bf16[48,768]{1,0:T(8,128)(2,1)S(1)}, bf16[48,768]{1,0:T(8,128)(2,1)S(1)}, u32[]{:S(2)}, u32[]{:S(2)}) collective-permute-start(bf16[48,768]{1,0:T(8,128)(2,1)S(1)} %get-tuple-element.18), channel_id=1, source_target_pairs={{0,64},{32,224},{64,0},{96,160},{128,192},{160,96},{192,128},{224,... | collective-permute-start | bytes 221192 | tf_op jit(solution)/shard_map/ppermute | solution.py:167
  89.2 18.4 %collective-permute-start.6 = (bf16[48,768]{1,0:T(8,128)(2,1)S(1)}, bf16[48,768]{1,0:T(8,128)(2,1)S(1)}, u32[]{:S(2)}, u32[]{:S(2)}) collective-permute-start(bf16[48,768]{1,0:T(8,128)(2,1)S(1)} %add_convert_fusion.1), channel_id=1, source_target_pairs={{0,192},{32,96},{64,128},{96,32},{128,64},{160,224},{192,0},{224,1... | collective-permute-start | bytes 221192 | tf_op jit(solution)/shard_map/ppermute | solution.py:167
  105.0 15.5 %collective-permute-start.3 = (bf16[32,1536]{1,0:T(8,128)(2,1)S(1)}, bf16[32,1536]{1,0:T(8,128)(2,1)S(1)}, u32[]{:S(2)}, u32[]{:S(2)}) collective-permute-start(bf16[32,1536]{1,0:T(8,128)(2,1)S(1)} %slice.51), channel_id=1, source_target_pairs={{0,4},{1,5},{2,6},{3,7},{4,0},{5,1},{6,2},{7,3},{8,12},{9,13},{10,... | collective-permute-start | bytes 294920 | tf_op jit(solution)/shard_map/ppermute | solution.py:170

commit v5 on v2

--- a/solution.py
+++ b/solution.py
@@ -166,18 +166,19 @@
             keep, away = total[:n], total[n:].astype(bf)
     input_grad = total.astype(bf)
 
-    got = lax.all_to_all(dw, "x", 0, 0)
-    total = jnp.sum(got.astype(f32), axis=0)
-    for step in range(2):
-        n = total.shape[0] // 2
-        keep, away = total[:n], total[n:].astype(bf)
+    def swap_zh(chunk, step):
         pairs = []
         for z in range(4):
             for c in range(2):
                 partner = (z ^ 1) if step == c else 3 - z
                 pairs.append((2 * z + c, 2 * partner + c))
-        got = lax.ppermute(away, ("zh", "c"), pairs)
-        total = keep + got.astype(f32)
+        return lax.ppermute(chunk.astype(bf), ("zh", "c"), pairs).astype(f32)
+
+    total = jnp.sum(lax.all_to_all(dw, "x", 0, 0).astype(f32), axis=0)
+    own, passed, straight, relay = [total[i * BLOCK : (i + 1) * BLOCK] for i in range(4)]
+    relayed = swap_zh(relay, 0)
+    own = own + swap_zh(straight, 0)
+    total = own + swap_zh(passed + relayed, 1)
     return input_grad, total.reshape(BLOCK, 2, cols // 2)
 
 

time: 120 us -> 118 us (0.983)
  the two profiles are of different devices: /device:TPU:96 before, /device:TPU:1 now
where the time goes in v5:
time: 118 us; the launch traced here: 115 us
  starting transfers between devices  57.6 us (49%)
  waiting for transfers between devices  32 us (27%)
  blocking collectives  9.49 us (8%)
  local copies, waits for them, and re-layouts  7.89 us (7%)
  Pallas kernels  5.06 us (4%)
  other arithmetic  2.37 us (2%)
    ppermute x3, starting transfers between devices, swap_zh(): return lax.ppermute(chunk.astype(bf), ('zh', 'c'), pairs).astype(f32)  24.4 us
    ppermute x1, starting transfers between devices, per_device(): got = lax.ppermute(other, 'c', [(0, 1), (1, 0)])  16.8 us
    ppermute x3, waiting for transfers between devices, swap_zh(): return lax.ppermute(chunk.astype(bf), ('zh', 'c'), pairs).astype(f32)  9.99 us
    all_to_all x1, blocking collectives, per_device(): d = lax.all_to_all(d_mine, 'mx', 0, 0)  9.49 us
    ppermute x3, waiting for transfers between devices, per_device(): got = lax.ppermute(away, 'my', [(i, i ^ bit) for i in range(8)])  9 us
    all_to_all x1, waiting for transfers between devices, per_device(): total = jnp.sum(lax.all_to_all(dw, 'x', 0, 0).astype(f32), axis=0)  8.54 us
    ppermute x3, starting transfers between devices, per_device(): got = lax.ppermute(away, 'my', [(i, i ^ bit) for i in range(8)])  7.84 us
    unnamed x14, local copies, waits for them, and re-layouts  7.1 us
  transfers between devices with their start and end apart: 9, of which 5 were waited for; matrix products, arithmetic and copies ran while one was open for 4% of the time, Pallas kernels for 2%

profile of v5, /device:TPU:1, one launch (start us, length us, event | category | flops | bytes accessed | tf_op | source)
XLA Modules:
  0.0 115.3 jit_solution(14812967521061448915)
XLA Ops:
  0.6 2.2 %copy.6 = bf16[192,8,2,384]{3,1,2,0:T(8,128)(2,1)S(1)} copy(bf16[192,8,2,384]{3,2,1,0:T(2,128)(2,1)} %bitcast.12) | data formatting | bytes 4718592
  2.9 1.4 %shard_map.59 = (bf16[4,64,768]{2,1,0:T(8,128)(2,1)S(1)}, bf16[16,768]{1,0:T(8,128)(2,1)S(1)}) custom-call(bf16[256,1536]{1,0:T(8,128)(2,1)S(1)} %copy-done, f32[2,128]{1,0:T(2,128)S(1)} %bitcast.9, bf16[1536,768]{1,0:T(8,128)(2,1)S(1)} %bitcast.6), custom_call_target="tpu_custom_call" | custom-call | flops 603979776 | bytes 4194304 | tf_op jit(solution)/shard_map/pallas_call | solution.py:147
  4.3 0.8 copy-done.2
  5.6 5.0 %all-to-all-start = ((bf16[4,64,768]{2,1,0:T(8,128)(2,1)}), bf16[4,64,768]{2,1,0:T(8,128)(2,1)S(1)}, u32[]{:S(2)}, u32[]{:S(2)}) async-start(bf16[4,64,768]{2,1,0:T(8,128)(2,1)} %copy-done.2), calls=%async_computation | async-start | bytes 786432 | tf_op jit(solution)/shard_map/all_to_all | solution.py:148
  10.6 1.8 %copy.7 = bf16[32,8,2,384]{3,1,2,0:T(8,128)(2,1)} copy(bf16[32,8,2,384]{3,2,1,0:T(2,128)(2,1)} %bitcast.13) | data formatting | bytes 786432
  12.4 4.4 %all-to-all-done.parts_ref = bf16[4,64,768]{2,1,0:T(8,128)(2,1)S(1)} async-done(((bf16[4,64,768]{2,1,0:T(8,128)(2,1)}), bf16[4,64,768]{2,1,0:T(8,128)(2,1)S(1)}, u32[]{:S(2)}, u32[]{:S(2)}) %all-to-all-start) | async-done | bytes 393248 | tf_op jit(solution)/shard_map/all_to_all | solution.py:148
  16.9 1.0 copy-done.1
  19.1 9.5 %all_to_all.15.d_ref = bf16[4,80,768]{2,1,0:T(8,128)(2,1)S(1)} all-to-all(bf16[4,80,768]{2,1,0:T(8,128)(2,1)S(1)} %shard_map.60), channel_id=1, replica_groups=mesh['x'=4,'zh'=4,'c'=2,'mx'=4,'my'=8] {'mx'}, dimensions={0} | all-to-all | bytes 983040 | tf_op jit(solution)/shard_map/all_to_all | solution.py:150
  28.5 1.4 %shard_map.62 = (bf16[768,768]{1,0:T(8,128)(2,1)S(1)}, bf16[768,768]{1,0:T(8,128)(2,1)S(1)}) custom-call(bf16[4,80,768]{2,1,0:T(8,128)(2,1)S(1)} %all_to_all.15.d_ref, bf16[256,1536]{1,0:T(8,128)(2,1)S(1)} %copy-done, f32[2,128]{1,0:T(2,128)S(1)} %bitcast.10), custom_call_target="tpu_custom_call" | custom-call | flops 603979776 | bytes 4194304 | tf_op jit(solution)/shard_map/pallas_call | solution.py:152
  30.0 16.8 %collective-permute-start.3 = (bf16[768,768]{1,0:T(8,128)(2,1)S(1)}, bf16[768,768]{1,0:T(8,128)(2,1)S(1)}, u32[]{:S(2)}, u32[]{:S(2)}) collective-permute-start(bf16[768,768]{1,0:T(8,128)(2,1)S(1)} %get-tuple-element.13), channel_id=1, source_target_pairs={{0,32},{32,0},{1,33},{33,1},{2,34},{34,2},{3,35},{35,3},{4,36},{36... | collective-permute-start | bytes 3538952 | tf_op jit(solution)/shard_map/ppermute | solution.py:155
  46.8 1.8 %shard_map.61 = (bf16[128,1536]{1,0:T(8,128)(2,1)S(1)}, bf16[128,1536]{1,0:T(8,128)(2,1)}) custom-call(bf16[4,80,768]{2,1,0:T(8,128)(2,1)S(1)} %all_to_all.15.d_ref, bf16[1536,768]{1,0:T(8,128)(2,1)S(1)} %bitcast.7, bf16[256,1536]{1,0:T(8,128)(2,1)S(1)} %copy-done, f32[2,128]{1,0:T(2,128)S(1)} %bitcast.11), custom_call_target="tpu_custom_call" | custom-call | flops 603979776 | bytes 4194304 | tf_op jit(solution)/shard_map/pallas_call | solution.py:156
  48.6 1.9 %collective-permute-start = (bf16[128,1536]{1,0:T(8,128)(2,1)}, bf16[128,1536]{1,0:T(8,128)(2,1)S(1)}, u32[]{:S(2)}, u32[]{:S(2)}) collective-permute-start(bf16[128,1536]{1,0:T(8,128)(2,1)} %get-tuple-element.11), channel_id=1, source_target_pairs={{0,1},{1,0},{2,3},{3,2},{4,5},{5,4},{6,7},{7,6},{8,9},{9,8},{10,11... | collective-permute-start | bytes 1179656 | tf_op jit(solution)/shard_map/ppermute | solution.py:162
  50.6 1.3 %add_convert_fusion = bf16[768,768]{1,0:T(8,128)(2,1)} fusion(bf16[768,768]{1,0:T(8,128)(2,1)S(1)} %collective-permute-done.3, bf16[768,768]{1,0:T(8,128)(2,1)S(1)} %get-tuple-element.12), kind=kLoop, calls=%fused_computation.1 | loop fusion | flops 2359296 | bytes 3538944 | tf_op jit(solution)/shard_map/convert_element_type | solution.py:159
  51.9 3.5 %all-to-all-start.2 = ((bf16[4,192,768]{2,1,0:T(8,128)(2,1)}), bf16[4,192,768]{2,1,0:T(8,128)(2,1)S(1)}, u32[]{:S(2)}, u32[]{:S(2)}) async-start(bf16[4,192,768]{2,1,0:T(8,128)(2,1)} %bitcast.1), calls=%async_computation.2 | async-start | bytes 2359296 | tf_op jit(solution)/shard_map/all_to_all | solution.py:177
  55.4 6.0 %collective-permute-done = bf16[128,1536]{1,0:T(8,128)(2,1)S(1)} collective-permute-done((bf16[128,1536]{1,0:T(8,128)(2,1)}, bf16[128,1536]{1,0:T(8,128)(2,1)S(1)}, u32[]{:S(2)}, u32[]{:S(2)}) %collective-permute-start) | collective-permute-done | bytes 393248 | tf_op jit(solution)/shard_map/ppermute | solution.py:162
  61.6 1.9 %collective-permute-start.1 = (bf16[64,1536]{1,0:T(8,128)(2,1)S(1)}, bf16[64,1536]{1,0:T(8,128)(2,1)S(1)}, u32[]{:S(2)}, u32[]{:S(2)}) collective-permute-start(bf16[64,1536]{1,0:T(8,128)(2,1)S(1)} %slice.56), channel_id=1, source_target_pairs={{0,2},{1,3},{2,0},{3,1},{4,6},{5,7},{6,4},{7,5},{8,10},{9,11},{10,... | collective-permute-start | bytes 589832 | tf_op jit(solution)/shard_map/ppermute | solution.py:162
  63.5 8.5 %all-to-all-done.2 = bf16[4,192,768]{2,1,0:T(8,128)(2,1)S(1)} async-done(((bf16[4,192,768]{2,1,0:T(8,128)(2,1)}), bf16[4,192,768]{2,1,0:T(8,128)(2,1)S(1)}, u32[]{:S(2)}, u32[]{:S(2)}) %all-to-all-start.2) | async-done | bytes 1179680 | tf_op jit(solution)/shard_map/all_to_all | solution.py:177
  72.3 12.0 %collective-permute-start.5 = (bf16[48,768]{1,0:T(8,128)(2,1)S(1)}, bf16[48,768]{1,0:T(8,128)(2,1)S(1)}, u32[]{:S(2)}, u32[]{:S(2)}) collective-permute-start(bf16[48,768]{1,0:T(8,128)(2,1)S(1)} %get-tuple-element.15), channel_id=1, source_target_pairs={{0,64},{32,224},{64,0},{96,160},{128,192},{160,96},{192,128},{224,... | collective-permute-start | bytes 221192 | tf_op jit(solution)/shard_map/ppermute | solution.py:175
  84.4 4.0 %collective-permute-start.2 = (bf16[32,1536]{1,0:T(8,128)(2,1)S(1)}, bf16[32,1536]{1,0:T(8,128)(2,1)S(1)}, u32[]{:S(2)}, u32[]{:S(2)}) collective-permute-start(bf16[32,1536]{1,0:T(8,128)(2,1)S(1)} %slice.57), channel_id=1, source_target_pairs={{0,4},{1,5},{2,6},{3,7},{4,0},{5,1},{6,2},{7,3},{8,12},{9,13},{10,... | collective-permute-start | bytes 294920 | tf_op jit(solution)/shard_map/ppermute | solution.py:162
  88.4 2.0 %collective-permute-start.4 = (bf16[48,768]{1,0:T(8,128)(2,1)S(1)}, bf16[48,768]{1,0:T(8,128)(2,1)S(1)}, u32[]{:S(2)}, u32[]{:S(2)}) collective-permute-start(bf16[48,768]{1,0:T(8,128)(2,1)S(1)} %get-tuple-element.14), channel_id=1, source_target_pairs={{0,64},{32,224},{64,0},{96,160},{128,192},{160,96},{192,128},{224,... | collective-permute-start | bytes 221192 | tf_op jit(solution)/shard_map/ppermute | solution.py:175
  90.4 10.4 %collective-permute-start.6 = (bf16[48,768]{1,0:T(8,128)(2,1)S(1)}, bf16[48,768]{1,0:T(8,128)(2,1)S(1)}, u32[]{:S(2)}, u32[]{:S(2)}) collective-permute-start(bf16[48,768]{1,0:T(8,128)(2,1)S(1)} %fusion.1), channel_id=1, source_target_pairs={{0,192},{32,96},{64,128},{96,32},{128,64},{160,224},{192,0},{224,1... | collective-permute-start | bytes 221192 | tf_op jit(solution)/shard_map/ppermute | solution.py:175
  100.9 3.0 %collective-permute-done.2 = bf16[32,1536]{1,0:T(8,128)(2,1)S(1)} collective-permute-done((bf16[32,1536]{1,0:T(8,128)(2,1)S(1)}, bf16[32,1536]{1,0:T(8,128)(2,1)S(1)}, u32[]{:S(2)}, u32[]{:S(2)}) %collective-permute-start.2) | collective-permute-done | bytes 98336 | tf_op jit(solution)/shard_map/ppermute | solution.py:162
  104.5 10.0 %collective-permute-done.6 = bf16[48,768]{1,0:T(8,128)(2,1)S(1)} collective-permute-done((bf16[48,768]{1,0:T(8,128)(2,1)S(1)}, bf16[48,768]{1,0:T(8,128)(2,1)S(1)}, u32[]{:S(2)}, u32[]{:S(2)}) %collective-permute-start.6) | collective-permute-done | bytes 73760 | tf_op jit(solution)/shard_map/ppermute | solution.py:175
  114.5 0.7 reshape.23
  (25 shorter events, 2.9 us)
Async XLA Ops:
  0.6 2.2 %copy-start = (bf16[256,1536]{1,0:T(8,128)(2,1)S(1)}, bf16[256,1536]{1,0:T(8,128)(2,1)}, u32[]{:S(2)}) copy-start(bf16[256,1536]{1,0:T(8,128)(2,1)} %x_ref.5) | copy-start | bytes 2359300
  0.6 2.2 %copy-start.5 = (f32[256]{0:T(256)S(1)}, f32[256]{0:T(256)}, u32[]{:S(2)}) copy-start(f32[256]{0:T(256)} %param.5) | copy-start | bytes 3076
  4.2 0.8 copy-start.2
  5.0 0.6 copy-start.3
  5.6 11.2 %all-to-all-start = ((bf16[4,64,768]{2,1,0:T(8,128)(2,1)}), bf16[4,64,768]{2,1,0:T(8,128)(2,1)S(1)}, u32[]{:S(2)}, u32[]{:S(2)}) async-start(bf16[4,64,768]{2,1,0:T(8,128)(2,1)} %copy-done.2), calls=%async_computation | async-start | bytes 786432 | tf_op jit(solution)/shard_map/all_to_all | solution.py:148
  16.9 1.0 copy-start.1
  17.9 0.7 copy-start.4
  30.0 20.6 %collective-permute-start.3 = (bf16[768,768]{1,0:T(8,128)(2,1)S(1)}, bf16[768,768]{1,0:T(8,128)(2,1)S(1)}, u32[]{:S(2)}, u32[]{:S(2)}) collective-permute-start(bf16[768,768]{1,0:T(8,128)(2,1)S(1)} %get-tuple-element.13), channel_id=1, source_target_pairs={{0,32},{32,0},{1,33},{33,1},{2,34},{34,2},{3,35},{35,3},{4,36},{36... | collective-permute-start | bytes 3538952 | tf_op jit(solution)/shard_map/ppermute | solution.py:155
  48.6 12.8 %collective-permute-start = (bf16[128,1536]{1,0:T(8,128)(2,1)}, bf16[128,1536]{1,0:T(8,128)(2,1)S(1)}, u32[]{:S(2)}, u32[]{:S(2)}) collective-permute-start(bf16[128,1536]{1,0:T(8,128)(2,1)} %get-tuple-element.11), channel_id=1, source_target_pairs={{0,1},{1,0},{2,3},{3,2},{4,5},{5,4},{6,7},{7,6},{8,9},{9,8},{10,11... | collective-permute-start | bytes 1179656 | tf_op jit(solution)/shard_map/ppermute | solution.py:162
  51.9 20.2 %all-to-all-start.2 = ((bf16[4,192,768]{2,1,0:T(8,128)(2,1)}), bf16[4,192,768]{2,1,0:T(8,128)(2,1)S(1)}, u32[]{:S(2)}, u32[]{:S(2)}) async-start(bf16[4,192,768]{2,1,0:T(8,128)(2,1)} %bitcast.1), calls=%async_computation.2 | async-start | bytes 2359296 | tf_op jit(solution)/shard_map/all_to_all | solution.py:177
  61.6 22.7 %collective-permute-start.1 = (bf16[64,1536]{1,0:T(8,128)(2,1)S(1)}, bf16[64,1536]{1,0:T(8,128)(2,1)S(1)}, u32[]{:S(2)}, u32[]{:S(2)}) collective-permute-start(bf16[64,1536]{1,0:T(8,128)(2,1)S(1)} %slice.56), channel_id=1, source_target_pairs={{0,2},{1,3},{2,0},{3,1},{4,6},{5,7},{6,4},{7,5},{8,10},{9,11},{10,... | collective-permute-start | bytes 589832 | tf_op jit(solution)/shard_map/ppermute | solution.py:162
  72.3 18.1 %collective-permute-start.5 = (bf16[48,768]{1,0:T(8,128)(2,1)S(1)}, bf16[48,768]{1,0:T(8,128)(2,1)S(1)}, u32[]{:S(2)}, u32[]{:S(2)}) collective-permute-start(bf16[48,768]{1,0:T(8,128)(2,1)S(1)} %get-tuple-element.15), channel_id=1, source_target_pairs={{0,64},{32,224},{64,0},{96,160},{128,192},{160,96},{192,128},{224,... | collective-permute-start | bytes 221192 | tf_op jit(solution)/shard_map/ppermute | solution.py:175
  84.4 19.4 %collective-permute-start.2 = (bf16[32,1536]{1,0:T(8,128)(2,1)S(1)}, bf16[32,1536]{1,0:T(8,128)(2,1)S(1)}, u32[]{:S(2)}, u32[]{:S(2)}) collective-permute-start(bf16[32,1536]{1,0:T(8,128)(2,1)S(1)} %slice.57), channel_id=1, source_target_pairs={{0,4},{1,5},{2,6},{3,7},{4,0},{5,1},{6,2},{7,3},{8,12},{9,13},{10,... | collective-permute-start | bytes 294920 | tf_op jit(solution)/shard_map/ppermute | solution.py:162
  88.4 16.1 %collective-permute-start.4 = (bf16[48,768]{1,0:T(8,128)(2,1)S(1)}, bf16[48,768]{1,0:T(8,128)(2,1)S(1)}, u32[]{:S(2)}, u32[]{:S(2)}) collective-permute-start(bf16[48,768]{1,0:T(8,128)(2,1)S(1)} %get-tuple-element.14), channel_id=1, source_target_pairs={{0,64},{32,224},{64,0},{96,160},{128,192},{160,96},{192,128},{224,... | collective-permute-start | bytes 221192 | tf_op jit(solution)/shard_map/ppermute | solution.py:175
  90.4 24.0 %collective-permute-start.6 = (bf16[48,768]{1,0:T(8,128)(2,1)S(1)}, bf16[48,768]{1,0:T(8,128)(2,1)S(1)}, u32[]{:S(2)}, u32[]{:S(2)}) collective-permute-start(bf16[48,768]{1,0:T(8,128)(2,1)S(1)} %fusion.1), channel_id=1, source_target_pairs={{0,192},{32,96},{64,128},{96,32},{128,64},{160,224},{192,0},{224,1... | collective-permute-start | bytes 221192 | tf_op jit(solution)/shard_map/ppermute | solution.py:175
